TPU v7x, 32 devices: a whole 2x2x4 slice. The times are simulated.
32 devices in a mesh: dp: 32 (over z, y, x, core).
Axes of the slice: x: 2, y: 2, z: 4, core: 2. Of those that a mesh axis runs over, the one named last changes fastest.
Arguments:
- tokens: float32 [8192, 1024], P('dp'), may hold values from -6 to 6
- cotangent: float32 [8192, 1024], P('dp'), may hold values from -6 to 6
- weight: float32 [1024, 1024], replicated, may hold values from -0.1875 to 0.1875
- first_moment: float32 [1024, 1024], P('dp'), may hold values from -0.6 to 0.6
- second_moment: float32 [1024, 1024], P('dp'), may hold values from 0.001 to 0.1
Outputs:
- projected: float32 [8192, 1024], P('dp')
- input_grad: float32 [8192, 1024], P('dp')
- new_weight: float32 [1024, 1024], replicated
- new_first: float32 [1024, 1024], P('dp')
- new_second: float32 [1024, 1024], P('dp')
- next_projected: float32 [8192, 1024], P('dp')
All inputs are finite; a program needn't handle non-finite values.
Results may differ from a plain program's by a relative error of at most 0.00017.
Values sent between devices are 32-bit elements; how exact they have to be, the bound alone decides.
No kernel may reach another device: no remote copies, remote signals or barrier semaphores. Data moves between devices by JAX's collectives and lax.ppermute only.
A program may use at most 64 MiB of HBM per device.

v0:
```python
import jax
import jax.numpy as jnp
from jax import lax
from jax.sharding import PartitionSpec as P

beta_one = 0.9
beta_two = 0.999
rate_value = 0.01
step_count = 10
adam_epsilon = 1e-08
norm_epsilon = 1e-06


def swapped(block, axis, stride):
    count = lax.axis_size(axis)
    route = []
    for low in range(count):
        high = low | 1 << stride
        if high != low and high < count:
            route += [(low, high), (high, low)]
    return lax.ppermute(block, axis, route)


def combine(left_rows, right_rows):
    cross_term = jnp.sum(left_rows * right_rows, axis=-1, keepdims=True)
    left_norm = jnp.sum(left_rows * left_rows, axis=-1, keepdims=True)
    right_norm = jnp.sum(right_rows * right_rows, axis=-1, keepdims=True)
    left_coef = 1.0 - cross_term / (2.0 * (left_norm + norm_epsilon))
    right_coef = 1.0 - cross_term / (2.0 * (right_norm + norm_epsilon))
    return left_coef * left_rows + right_coef * right_rows


def adam_update(gradient, weight_rows, first_rows, second_rows):
    first_new = beta_one * first_rows + (1.0 - beta_one) * gradient
    second_new = beta_two * second_rows + (1.0 - beta_two) * gradient * gradient
    first_hat = first_new / (1.0 - beta_one**step_count)
    second_hat = second_new / (1.0 - beta_two**step_count)
    weight_new = weight_rows - rate_value * first_hat / (jnp.sqrt(second_hat) + adam_epsilon)
    return (weight_new, first_new, second_new)


def on_device(tokens, cotangent, weight, first_moment, second_moment):
    highest = lax.Precision.HIGHEST
    projected = jnp.dot(tokens, weight, precision=highest, preferred_element_type=jnp.float32)
    input_grad = lax.dot_general(
        cotangent,
        weight,
        (((1,), (1,)), ((), ())),
        precision=highest,
        preferred_element_type=jnp.float32,
    )
    token_count = tokens.shape[0]
    model_width = weight.shape[0]
    devices = lax.axis_size("dp")
    levels = devices.bit_length() - 1
    index = lax.axis_index("dp")

    def row_grad(start, count):
        columns = lax.dynamic_slice_in_dim(tokens, start, count, 1)
        product = lax.dot_general(
            columns,
            cotangent,
            (((0,), (0,)), ((), ())),
            precision=highest,
            preferred_element_type=jnp.float32,
        )
        return product / token_count

    current = None
    for level in range(levels):
        bit = levels - 1 - level
        halfway = model_width >> level + 1
        upper = index >> bit & 1
        keep_start = upper * halfway
        send_start = (1 - upper) * halfway
        if current is None:
            outgoing = row_grad(send_start, halfway)
        else:
            outgoing = lax.dynamic_slice_in_dim(current, send_start, halfway, 0)
        received = swapped(outgoing, "dp", bit)
        if current is None:
            kept = row_grad(keep_start, halfway)
        else:
            kept = lax.dynamic_slice_in_dim(current, keep_start, halfway, 0)
        current = combine(kept, received)
    own_rows = current.shape[0]
    row_start = index * own_rows
    weight_rows = lax.dynamic_slice_in_dim(weight, row_start, own_rows, 0)
    weight_new, new_first, new_second = adam_update(
        current, weight_rows, first_moment, second_moment
    )
    new_weight = lax.all_gather(weight_new, "dp", axis=0, tiled=True)
    next_projected = jnp.dot(
        tokens, new_weight, precision=highest, preferred_element_type=jnp.float32
    )
    return (projected, input_grad, new_weight, new_first, new_second, next_projected)


def solution(mesh):
    placed = (P("dp", None), P("dp", None), P(), P("dp", None), P("dp", None))
    return jax.shard_map(
        on_device,
        mesh=mesh,
        in_specs=placed,
        out_specs=(P("dp", None), P("dp", None), P(), P("dp", None), P("dp", None), P("dp", None)),
        check_vma=False,
    )
```

profile of v0, /device:TPU:0, one launch (start us, length us, event | category | flops | bytes accessed | tf_op | source)
XLA Modules:
  0.0 254.7 jit_solution(9720307779371533838)
XLA Ops:
  7.2 1.2 copy-done
  8.4 4.4 %convolution_multiply_fusion = f32[512,1024]{1,0:T(8,128)} fusion(f32[256,1024]{1,0:T(8,128)} %param.6, f32[256,1024]{1,0:T(8,128)S(1)} %copy-done, s32[]{:T(128)S(6)} %select_n.35), kind=kOutput, calls=%fused_computation.4 | convolution fusion | flops 1611137024 | bytes 3670020 | tf_op jit(solution)/shard_map/dot_general | solution.py:60
  12.8 4.0 %collective-permute-start = (f32[512,1024]{1,0:T(8,128)}, f32[512,1024]{1,0:T(8,128)}, u32[]{:S(2)}, u32[]{:S(2)}) collective-permute-start(f32[512,1024]{1,0:T(8,128)} %convolution_multiply_fusion), channel_id=1, source_target_pairs={{0,16},{16,0},{1,17},{17,1},{2,18},{18,2},{3,19},{19,3},{4,20},{20... | collective-permute-start | bytes 6291464 | tf_op jit(solution)/shard_map/ppermute | solution.py:21
  16.8 90.9 %collective-permute-done = f32[512,1024]{1,0:T(8,128)} collective-permute-done((f32[512,1024]{1,0:T(8,128)}, f32[512,1024]{1,0:T(8,128)}, u32[]{:S(2)}, u32[]{:S(2)}) %collective-permute-start) | collective-permute-done | bytes 2097184 | tf_op jit(solution)/shard_map/ppermute | solution.py:21
  107.7 4.0 %multiply_reduce_fusion.1 = (f32[512]{0:T(512)S(1)}, f32[512]{0:T(512)S(1)}, f32[512]{0:T(512)S(1)}, f32[512,1024]{1,0:T(8,128)S(1)}) fusion(f32[512,1024]{1,0:T(8,128)} %collective-permute-done, f32[256,1024]{1,0:T(8,128)S(1)} %copy-done.2, f32[256,1024]{1,0:T(8,128)S(1)} %copy-done, s32[]{:T(128)S(6)} %select_n.34), kind=kOutput, calls=%fused_computation.2 | convolution fusion | flops 1614281216 | bytes 5773316 | tf_op jit(solution)/shard_map/dot_general | solution.py:60
  111.7 1.9 multiply_add_fusion
  113.7 1.0 constant_dynamic-slice_fusion.3
  115.4 23.9 %collective-permute-done.1 = f32[256,1024]{1,0:T(8,128)} collective-permute-done((f32[256,1024]{1,0:T(8,128)}, f32[256,1024]{1,0:T(8,128)}, u32[]{:S(2)}, u32[]{:S(2)}) %collective-permute-start.1) | collective-permute-done | bytes 1048608 | tf_op jit(solution)/shard_map/ppermute | solution.py:21
  139.4 1.5 multiply_reduce_fusion.4
  140.9 1.4 multiply_add_fusion.1
  143.3 1.3 collective-permute-start.2
  144.7 10.9 %collective-permute-done.2 = f32[128,1024]{1,0:T(8,128)S(1)} collective-permute-done((f32[128,1024]{1,0:T(8,128)S(1)}, f32[128,1024]{1,0:T(8,128)S(1)}, u32[]{:S(2)}, u32[]{:S(2)}) %collective-permute-start.2) | collective-permute-done | bytes 524320 | tf_op jit(solution)/shard_map/ppermute | solution.py:21
  155.6 1.2 multiply_reduce_fusion.7
  156.9 1.2 multiply_add_fusion.2
  158.1 1.4 collective-permute-start.3
  159.5 5.1 %collective-permute-done.3 = f32[64,1024]{1,0:T(8,128)S(1)} collective-permute-done((f32[64,1024]{1,0:T(8,128)S(1)}, f32[64,1024]{1,0:T(8,128)S(1)}, u32[]{:S(2)}, u32[]{:S(2)}) %collective-permute-start.3) | collective-permute-done | bytes 262176 | tf_op jit(solution)/shard_map/ppermute | solution.py:21
  165.0 1.3 collective-permute-done.4
  166.5 1.8 divide_subtract_fusion
  168.3 7.0 %fusion.16 = f32[256,1024]{1,0:T(8,128)} fusion(f32[256,1024]{1,0:T(8,128)S(1)} %copy-done, f32[1024,1024]{1,0:T(8,128)} %param.7), kind=kOutput, calls=%fused_computation.55 | convolution fusion | flops 3221225472 | bytes 6291456 | tf_op jit(solution)/shard_map/dot_general | solution.py:44
  175.3 4.9 %fusion.17 = f32[256,1024]{1,0:T(8,128)} fusion(f32[256,1024]{1,0:T(8,128)S(1)} %copy-done.3, f32[1024,1024]{1,0:T(8,128)S(1)} %copy-done.1), kind=kOutput, calls=%fused_computation.56 | convolution fusion | flops 3221225472 | bytes 6291456 | tf_op jit(solution)/shard_map/dot_general | solution.py:45
  180.2 53.1 %all-gather.2.cloned.1.call-done = f32[1024,1024]{1,0:T(8,128)} async-done(((f32[32,1024]{1,0:T(8,128)}), f32[1024,1024]{1,0:T(8,128)}) %all-gather.2.cloned.1.call-update) | async-done | bytes 4194320 | tf_op jit(solution)/shard_map/all_gather | solution.py:92
  233.3 8.5 %convolution_bitcast_fusion = f32[256,1024]{0,1:T(8,128)S(1)} fusion(f32[1024,1024]{1,0:T(8,128)} %all-gather.2.cloned.1.call-done, f32[256,1024]{1,0:T(8,128)S(1)} %copy-done), kind=kOutput, calls=%fused_computation.5 | convolution fusion | flops 3221225472 | bytes 6291456 | tf_op jit(solution)/shard_map/dot_general | solution.py:93
  241.8 1.3 copy.11
  243.1 4.8 %copy.13 = f32[1024,1024]{1,0:T(8,128)} copy(f32[1024,1024]{1,0:T(8,128)} %all-gather.2.cloned.1.call-done) | data formatting | bytes 8388608
  (28 shorter events, 2.4 us)
Async XLA Ops:
  7.2 1.2 copy-start
  7.2 100.5 %copy-start.2 = (f32[256,1024]{1,0:T(8,128)S(1)}, f32[256,1024]{1,0:T(8,128)}, u32[]{:S(2)}) copy-start(f32[256,1024]{1,0:T(8,128)} %param.6) | copy-start | bytes 3145732
  7.2 226.1 %all-gather.2.cloned.1.call-start = ((), (), s32[]{:S(2)}) async-start(), calls=%async_computation | async-start | bytes 4325376 | tf_op jit(solution)/shard_map/all_gather | solution.py:92
  12.8 94.9 %collective-permute-start = (f32[512,1024]{1,0:T(8,128)}, f32[512,1024]{1,0:T(8,128)}, u32[]{:S(2)}, u32[]{:S(2)}) collective-permute-start(f32[512,1024]{1,0:T(8,128)} %convolution_multiply_fusion), channel_id=1, source_target_pairs={{0,16},{16,0},{1,17},{17,1},{2,18},{18,2},{3,19},{19,3},{4,20},{20... | collective-permute-start | bytes 6291464 | tf_op jit(solution)/shard_map/ppermute | solution.py:21
  114.7 24.7 %collective-permute-start.1 = (f32[256,1024]{1,0:T(8,128)}, f32[256,1024]{1,0:T(8,128)}, u32[]{:S(2)}, u32[]{:S(2)}) collective-permute-start(f32[256,1024]{1,0:T(8,128)} %constant_dynamic-slice_fusion.3), channel_id=1, source_target_pairs={{0,8},{8,0},{1,9},{9,1},{2,10},{10,2},{3,11},{11,3},{4,12},{12,4},... | collective-permute-start | bytes 3145736 | tf_op jit(solution)/shard_map/ppermute | solution.py:21
  142.3 1.0 copy-start.4
  143.3 12.3 %collective-permute-start.2 = (f32[128,1024]{1,0:T(8,128)S(1)}, f32[128,1024]{1,0:T(8,128)S(1)}, u32[]{:S(2)}, u32[]{:S(2)}) collective-permute-start(f32[128,1024]{1,0:T(8,128)S(1)} %constant_dynamic-slice_fusion.2), channel_id=1, source_target_pairs={{0,4},{4,0},{1,5},{5,1},{2,6},{6,2},{3,7},{7,3},{8,12},{12,8},{9,1... | collective-permute-start | bytes 1572872 | tf_op jit(solution)/shard_map/ppermute | solution.py:21
  156.8 9.7 %copy-start.5 = (f32[32,1024]{1,0:T(8,128)S(1)}, f32[32,1024]{1,0:T(8,128)}, u32[]{:S(2)}) copy-start(f32[32,1024]{1,0:T(8,128)} %param.8) | copy-start | bytes 393220
  156.8 9.7 %copy-start.6 = (f32[32,1024]{1,0:T(8,128)S(1)}, f32[32,1024]{1,0:T(8,128)}, u32[]{:S(2)}) copy-start(f32[32,1024]{1,0:T(8,128)} %param.9) | copy-start | bytes 393220
  158.1 6.4 %collective-permute-start.3 = (f32[64,1024]{1,0:T(8,128)S(1)}, f32[64,1024]{1,0:T(8,128)S(1)}, u32[]{:S(2)}, u32[]{:S(2)}) collective-permute-start(f32[64,1024]{1,0:T(8,128)S(1)} %constant_dynamic-slice_fusion.1), channel_id=1, source_target_pairs={{0,2},{2,0},{1,3},{3,1},{4,6},{6,4},{5,7},{7,5},{8,10},{10,8},{9,1... | collective-permute-start | bytes 786440 | tf_op jit(solution)/shard_map/ppermute | solution.py:21
  164.9 1.4 collective-permute-start.4
  168.3 7.0 %copy-start.1 = (f32[1024,1024]{1,0:T(8,128)S(1)}, f32[1024,1024]{1,0:T(8,128)}, u32[]{:S(2)}) copy-start(f32[1024,1024]{1,0:T(8,128)} %param.7) | copy-start | bytes 12582916
  168.3 7.0 %copy-start.3 = (f32[256,1024]{1,0:T(8,128)S(1)}, f32[256,1024]{1,0:T(8,128)}, u32[]{:S(2)}) copy-start(f32[256,1024]{1,0:T(8,128)} %param.6) | copy-start | bytes 3145732
Sparse Core Ops, SparseCore 0:
  168.4 64.8 all-gather.1
where the time goes:
time: 255 us
  waiting for transfers between devices  185 us (73%)
  matrix products  28.7 us (11%)
  between operations  14.2 us (6%)
  other arithmetic  9.58 us (4%)
  local copies, waits for them, and re-layouts  9.38 us (4%)
  starting transfers between devices  7.56 us (3%)
    ppermute x5, waiting for transfers between devices, swapped(): return lax.ppermute(block, axis, route)  132 us
    all_gather x1, waiting for transfers between devices, on_device(): new_weight = lax.all_gather(weight_new, 'dp', axis=0, tiled=True)  53.1 us
    dot_general x1, matrix products, on_device(): jnp.dot(tokens, new_weight, precision=highest, preferred_element_type=jnp...  8.47 us
    dot_general x2, matrix products, row_grad(): lax.dot_general(columns, cotangent, (((0,), (0,)), ((), ())), precision=h...  8.4 us
    unnamed x16, local copies, waits for them, and re-layouts  8.25 us
    ppermute x5, starting transfers between devices, swapped(): return lax.ppermute(block, axis, route)  7.52 us
    dot_general x1, matrix products, on_device(): jnp.dot(tokens, weight, precision=highest, preferred_element_type=jnp.flo...  6.98 us
  transfers between devices with their start and end apart: 6, of which 6 were waited for; matrix products, arithmetic and copies ran while one was open for 5% of the time, Pallas kernels for 0%

commit v1 on v0

v1 whole, which is shorter than its diff:
```python
import functools
import jax
import jax.numpy as jnp
from jax import lax
from jax.experimental import pallas as pl
from jax.experimental.pallas import tpu as pltpu
from jax.sharding import PartitionSpec as P

beta_one = 0.9
beta_two = 0.999
rate_value = 0.01
step_count = 10
adam_epsilon = 1e-08
norm_epsilon = 1e-06

SIZES = (1,1,1,1)
FIRST_STREAM = 2

OWNER, TOP, MIDDLE, CORE, BITS = range(5)


def kernel_call(kernel, name, outs, megabytes, place, *arrays):
    vmem = pl.BlockSpec(memory_space=pltpu.VMEM)
    return pl.pallas_call(
        kernel,
        out_shape=tuple(outs),
        in_specs=[pl.BlockSpec(memory_space=pltpu.SMEM)] + [vmem] * len(arrays),
        out_specs=tuple(vmem for _ in outs),
        compiler_params=pltpu.CompilerParams(vmem_limit_bytes=megabytes << 20),
        cost_estimate=pl.CostEstimate(flops=1, bytes_accessed=1, transcendentals=0),
        name=name,
    )(place, *arrays)


def f32(*shape):
    return jax.ShapeDtypeStruct(shape, jnp.float32)


def bf16(*shape):
    return jax.ShapeDtypeStruct(shape, jnp.bfloat16)


def swapped(block, mask):
    count = lax.axis_size("dp")
    return lax.ppermute(block, "dp", [(i, i ^ mask) for i in range(count)])


def parts(x):
    high = x.astype(jnp.bfloat16)
    return high, (x - high.astype(jnp.float32)).astype(jnp.bfloat16)


def product(left, right, contract=0):
    left_high, left_low = left
    right_high, right_low = right

    def dot(a, b):
        return lax.dot_general(
            a, b, (((1,), (contract,)), ((), ())), preferred_element_type=jnp.float32
        )

    return dot(left_high, right_high) + (dot(left_high, right_low) + dot(left_low, right_high))


def combine(left_rows, right_rows):
    cross_term = jnp.sum(left_rows * right_rows, axis=-1, keepdims=True)
    left_norm = jnp.sum(left_rows * left_rows, axis=-1, keepdims=True)
    right_norm = jnp.sum(right_rows * right_rows, axis=-1, keepdims=True)
    left_coef = 1.0 - cross_term / (2.0 * (left_norm + norm_epsilon))
    right_coef = 1.0 - cross_term / (2.0 * (right_norm + norm_epsilon))
    return left_coef * left_rows + right_coef * right_rows


def adam_update(gradient, weight_rows, first_rows, second_rows):
    first_new = beta_one * first_rows + (1.0 - beta_one) * gradient
    second_new = beta_two * second_rows + (1.0 - beta_two) * gradient * gradient
    first_hat = first_new / (1.0 - beta_one**step_count)
    second_hat = second_new / (1.0 - beta_two**step_count)
    weight_new = weight_rows - rate_value * first_hat / (jnp.sqrt(second_hat) + adam_epsilon)
    return (weight_new, first_new, second_new)


def prepare_kernel(middle, own, spans, place_ref, tokens_ref, keep_ref, other_ref):
    def fill(mine):
        width = 128
        for base in range(0, tokens_ref.shape[1], width):
            block = tokens_ref[:, base : base + width].T
            for group in range(base // own, (base + width) // own):
                node, here = divmod(group, 2)
                top, mid = divmod(node, middle)
                target = keep_ref if here == mine else other_ref
                for first, piece in spans:
                    row = first * middle * 2 + (mid * 2 + top) * piece
                    low = group * own + first - base
                    target[row : row + piece, :] = block[low : low + piece, :]

    for mine in range(2):
        pl.when(place_ref[CORE] == mine)(functools.partial(fill, mine))


def choose_kernel(place_ref, cotangent_ref, swap_ref, send_ref):
    half = send_ref.shape[0]
    send_ref[...] = jnp.where(place_ref[OWNER] == 1, swap_ref[half:, :], cotangent_ref[:half, :])


def share_kernel(spans, place_ref, keep_ref, swap_ref, near_ref, *send_refs):
    owner = place_ref[OWNER] == 1
    near_ref[...] = jnp.where(owner, keep_ref[...], swap_ref[...])
    row = 0
    for send_ref in send_refs:
        rows = slice(row, row + send_ref.shape[0])
        send_ref[...] = jnp.where(owner, swap_ref[rows, :], keep_ref[rows, :])
        row += send_ref.shape[0]


def project_kernel(place_ref, tokens_ref, cotangent_ref, weight_ref, projected_ref, grad_ref):
    tokens = parts(tokens_ref[...])
    cotangent = parts(cotangent_ref[...])
    width = weight_ref.shape[0]
    step = min(256, width)
    for base in range(0, width, step):
        span = slice(base, base + step)
        projected_ref[:, span] = product(tokens, parts(weight_ref[:, span]))
        grad_ref[:, span] = product(cotangent, parts(weight_ref[span, :]), 1)


def near_kernel(scale, place_ref, tokens_ref, cotangent_ref, swap_ref, *near_refs):
    right = parts(jnp.where(place_ref[OWNER] == 1, cotangent_ref[...], swap_ref[...]))
    row = 0
    for near_ref in near_refs:
        rows = near_ref.shape[0]
        near_ref[...] = product(parts(tokens_ref[row : row + rows, :]), right) * scale
        row += rows


def assemble_kernel(place_ref, mine_ref, other_ref, high_ref, low_ref):
    owner = place_ref[OWNER] == 1
    half = mine_ref.shape[0]
    for at in range(2):
        chosen = jnp.where(owner == (at == 0), mine_ref[...], other_ref[...])
        rows = slice(at * half, (at + 1) * half)
        high_ref[rows, :], low_ref[rows, :] = parts(chosen)


def halves(place_ref, bit, half):
    mine = place_ref[BITS + bit]
    return [pl.ds(pl.multiple_of(part * half, half), half) for part in (mine, 1 - mine)]


def first_kernel(scale, bit, place_ref, near_ref, far_ref, high_ref, low_ref, keep_ref, send_ref):
    right = (high_ref[...], low_ref[...])
    for target, rows in zip((send_ref, keep_ref), halves(place_ref, bit, keep_ref.shape[0])[::-1]):
        target[...] = combine(near_ref[rows, :], product(parts(far_ref[rows, :]), right) * scale)


def middle_kernel(bit, place_ref, kept_ref, received_ref, keep_ref, send_ref):
    for target, rows in zip((send_ref, keep_ref), halves(place_ref, bit, keep_ref.shape[0])[::-1]):
        target[...] = combine(kept_ref[rows, :], received_ref[rows, :])


def merge_kernel(place_ref, kept_ref, received_ref, out_ref):
    out_ref[...] = combine(kept_ref[...], received_ref[...])


def last_kernel(
    first, place_ref, kept_ref, received_ref, weight_ref,
    own_first_ref, other_first_ref, own_second_ref, other_second_ref,
    weight_out, first_out, second_out,
):
    piece = first_out.shape[0]
    span = slice(first, first + piece)
    for top in range(2):
        mine = place_ref[TOP] == top
        rows = slice(top * piece, (top + 1) * piece)
        gradient = combine(kept_ref[rows, :], received_ref[rows, :])
        weight_new, first_new, second_new = adam_update(
            gradient,
            weight_ref[top, span, :],
            jnp.where(mine, own_first_ref[span, :], other_first_ref[span, :]),
            jnp.where(mine, own_second_ref[span, :], other_second_ref[span, :]),
        )
        weight_out[rows, :] = weight_new

        @pl.when(mine)
        def _():
            first_out[...] = first_new
            second_out[...] = second_new


def finish_kernel(middle, own, streams, place_ref, tokens_ref, *refs):
    *block_refs, weight_ref, projected_ref = refs
    mid, core = place_ref[MIDDLE], place_ref[CORE]
    for at, block_ref in enumerate(block_refs):
        stream, at = divmod(at, 2 * middle)
        far_mid, far_core = divmod(at, 2)
        device = (mid ^ far_mid) * 2 + (core ^ far_core)
        start = 0
        for first, piece in streams[stream]:
            for top in range(2):
                row = (device + top * middle * 2) * own + first
                weight_ref[pl.ds(pl.multiple_of(row, piece), piece), :] = block_ref[start : start + piece, :]
                start += piece
    depth = min(256, tokens_ref.shape[1])
    total = jnp.zeros(projected_ref.shape, jnp.float32)
    for base in range(0, tokens_ref.shape[1], depth):
        span = slice(base, base + depth)
        total = total + product(parts(tokens_ref[:, span]), parts(weight_ref[span, :]))
    projected_ref[...] = total


def tied(after, values):
    return list(lax.optimization_barrier((after, *values))[1:])


def chunk_order(sizes, levels):
    own = sum(sizes)
    fixed, ready, steps = 0.08 * own, {}, []
    free = [0.0] * levels
    for k, size in enumerate(sizes):
        ready[k, 0] = sum(sizes[: k + 1])
    for level in range(1, levels):
        cost = 1.0 if level == 1 else 0.5 if level == levels - 1 else 2.0 ** (1 - level)
        for k, size in enumerate(sizes):
            free[level] = max(free[level], ready[k, level - 1] + fixed) + cost * size
            ready[k, level] = free[level]
    return sorted(ready, key=lambda step: (ready[step], step[1]))


def relative_blocks(rows, order):
    blocks = {0: rows}
    for bit in order:
        for mask in list(blocks):
            blocks[mask | 1 << bit] = swapped(blocks[mask], 1 << bit)
    return blocks


def on_device(tokens, cotangent, weight, first_moment, second_moment):
    token_count, width = tokens.shape
    devices = lax.axis_size("dp")
    levels = devices.bit_length() - 1
    index = lax.axis_index("dp")
    own = width // devices
    middle = devices // 4
    quarter = own // 4
    sizes = [quarter * part for part in SIZES] if own % 32 == 0 else [own]
    spans = [(sum(sizes[:k]), sizes[k]) for k in range(len(sizes))]
    streams = [spans[:FIRST_STREAM], spans[FIRST_STREAM:]] if len(spans) > 1 else [spans]
    top_mask = devices >> 1
    core, top = index & 1, index >> levels - 1
    scale = 1.0 / token_count
    place = jnp.stack(
        [(core == top).astype(jnp.int32), top, index >> 1 & middle - 1, core]
        + [index >> bit & 1 for bit in range(levels)]
    )
    half_rows = width // 2

    cotangent_swap = swapped(cotangent, 1)
    tokens_keep, tokens_other = kernel_call(
        functools.partial(prepare_kernel, middle, own, spans), "prepare",
        [f32(half_rows, token_count)] * 2, 4, place, tokens,
    )
    tokens_swap = swapped(tokens_other, 1)
    (send_cotangent,) = kernel_call(
        choose_kernel, "choose", [f32(token_count // 2, width)], 4, place, cotangent, cotangent_swap
    )
    far_mine = swapped(send_cotangent, top_mask)
    near_tokens, *send_tokens = kernel_call(
        functools.partial(share_kernel, spans), "share",
        [f32(half_rows, token_count)] + [f32(2 * middle * piece, token_count) for _, piece in spans],
        4, place, tokens_keep, tokens_swap,
    )
    far_tokens = [swapped(block, top_mask) for block in send_tokens]
    other_first = swapped(first_moment, top_mask)
    other_second = swapped(second_moment, top_mask)

    near = kernel_call(
        functools.partial(near_kernel, scale), "near",
        [f32(2 * middle * piece, width) for _, piece in spans], 12, place, near_tokens, cotangent, cotangent_swap,
    )
    projected, input_grad = kernel_call(
        project_kernel, "project", [f32(token_count, width)] * 2, 20, place, tokens, cotangent, weight
    )
    weight_rows = lax.dynamic_index_in_dim(
        weight.reshape(2, devices // 2, own, width), index % (devices // 2), 1, keepdims=False
    )
    near, projected, input_grad, weight_rows, far_mine, far_tokens[0] = lax.optimization_barrier(
        (near, projected, input_grad, weight_rows, far_mine, far_tokens[0])
    )
    far_high, far_low = kernel_call(
        assemble_kernel, "assemble", [bf16(token_count, width)] * 2, 6, place, far_mine, swapped(far_mine, 1)
    )

    bits = list(range(levels - 2, 0, -1)) + [levels - 1]
    state, outs, after = {}, {}, far_high
    order = [(k, 0) for k in range(len(spans))] + [step for step in chunk_order(sizes, levels) if step[1] > 0]
    for at, (k, level) in enumerate(order):
        if at == len(spans):
            kept = [state[j][0] for j in range(len(spans))]
            after = lax.optimization_barrier(tuple(kept))[-1]
        if at == len(spans) + 2:
            after, other_first, other_second = lax.optimization_barrier((after, other_first, other_second))
        first, piece = spans[k]
        rows = 2 * piece * middle >> level + 1
        if level == 0:
            kernel, name, count = functools.partial(first_kernel, scale, bits[0]), "first", 2
            operands = [near[k], far_tokens[k], far_high, far_low]
        else:
            keep, send = state[k]
            operands = [keep, swapped(send, 1 << bits[level - 1])]
            if level < levels - 2:
                kernel, name, count = functools.partial(middle_kernel, bits[level]), "middle", 2
            elif level == levels - 2:
                kernel, name, count, rows = merge_kernel, "merge", 1, 2 * piece
        operands = tied(after, operands)
        if level < levels - 1:
            state[k] = kernel_call(kernel, name, [f32(rows, width)] * count, 8, place, *operands)
            state[k] = (state[k][0], state[k][-1])
            if level > 0:
                after = state[k][0]
        else:
            outs[k] = kernel_call(
                functools.partial(last_kernel, first), "last",
                [f32(2 * piece, width), f32(piece, width), f32(piece, width)], 4,
                place, *operands, weight_rows, first_moment, other_first, second_moment, other_second,
            )
            after = outs[k][0]
    outs = [outs[k] for k in range(len(spans))]
    new_rows, new_first, new_second = zip(*outs)
    new_first = jnp.concatenate(new_first, axis=0)
    new_second = jnp.concatenate(new_second, axis=0)

    if devices > 64:
        mine = jnp.concatenate(
            [lax.dynamic_slice_in_dim(x, top * (x.shape[0] // 2), x.shape[0] // 2, 0) for x in new_rows], axis=0
        )
        new_weight = lax.all_gather(mine, "dp", axis=0, tiled=True)
        next_projected = jnp.dot(
            tokens, new_weight, precision=lax.Precision.HIGH, preferred_element_type=jnp.float32
        )
        return (projected, input_grad, new_weight, new_first, new_second, next_projected)

    order = list(range(levels - 2, 0, -1))
    blocks = []
    for at, stream in enumerate(streams):
        rows = jnp.concatenate([new_rows[spans.index(span)] for span in stream], axis=0)
        found = relative_blocks(rows, order if at == 0 else order[::-1])
        for mid in range(middle):
            blocks += [found[mid << 1], swapped(found[mid << 1], 1)]
    new_weight, next_projected = kernel_call(
        functools.partial(finish_kernel, middle, own, streams), "finish",
        [f32(width, width), f32(token_count, width)], 28, place, tokens, *blocks,
    )
    return (projected, input_grad, new_weight, new_first, new_second, next_projected)


def solution(mesh):
    split, whole = P("dp", None), P()
    return jax.shard_map(
        on_device,
        mesh=mesh,
        in_specs=(split, split, whole, split, split),
        out_specs=(split, split, whole, split, split, split),
        check_vma=False,
    )
```

time: 255 us -> 142 us (0.56)
  waiting for transfers between devices: 185 us -> 42.3 us
  starting transfers between devices: 7.56 us -> 56.4 us
  Pallas kernels: 0 us -> 32.4 us
  matrix products: 28.7 us -> 0 us
  between operations: 14.2 us -> 0.98 us
  other arithmetic: 9.58 us -> 0.72 us
    ppermute x5 -> x56, waiting for transfers between devices: 132 us -> 42.3 us  [swapped(): return lax.ppermute(block, 'dp', [(i, i ^ mask) for i in range(count)])]
    all_gather x1 -> x0, waiting for transfers between devices: 53.1 us -> none  [on_device(): new_weight = lax.all_gather(weight_new, 'dp', axis=0, tiled=True)]
    ppermute x5 -> x56, starting transfers between devices: 7.52 us -> 56.4 us  [swapped(): return lax.ppermute(block, 'dp', [(i, i ^ mask) for i in range(count)])]
    pallas_call x0 -> x27, Pallas kernels: none -> 32.4 us  [kernel_call(): pl.pallas_call(kernel, out_shape=tuple(outs), in_specs=[pl.BlockSpec(memo...]
    dot_general x5 -> x0, matrix products: 28.7 us -> none  [the longest x1 8.47 us: on_device(): jnp.dot(tokens, new_weight, precision=highest, preferred_element_type=jnp...]
    add x4 -> x0, other arithmetic: 4.66 us -> none  [combine(): return left_coef * left_rows + right_coef * right_rows]
    reduce_sum x4 -> x0, other arithmetic: 3.07 us -> none  [combine(): left_norm = jnp.sum(left_rows * left_rows, axis=-1, keepdims=True)]
    unnamed x16 -> x28, local copies, waits for them, and re-layouts: 8.25 us -> 7.85 us
  transfers between devices with their start and end apart: 6 -> 56, of which waited for: 6 -> 20; matrix products, arithmetic and copies ran while one was open for 5% -> 1% of each run, Pallas kernels for 0% -> 20%
where the time goes in v1:
time: 142 us
  starting transfers between devices  56.4 us (40%)
  waiting for transfers between devices  42.3 us (30%)
  Pallas kernels  32.4 us (23%)
  local copies, waits for them, and re-layouts  8.92 us (6%)
    ppermute x56, starting transfers between devices, swapped(): return lax.ppermute(block, 'dp', [(i, i ^ mask) for i in range(count)])  56.4 us
    ppermute x56, waiting for transfers between devices, swapped(): return lax.ppermute(block, 'dp', [(i, i ^ mask) for i in range(count)])  42.3 us
    pallas_call x27, Pallas kernels, kernel_call(): pl.pallas_call(kernel, out_shape=tuple(outs), in_specs=[pl.BlockSpec(memo...  32.4 us
    unnamed x28, local copies, waits for them, and re-layouts  7.85 us
  transfers between devices with their start and end apart: 56, of which 20 were waited for; matrix products, arithmetic and copies ran while one was open for 1% of the time, Pallas kernels for 20%

profile of v1, /device:TPU:0, one launch (start us, length us, event | category | flops | bytes accessed | tf_op | source)
XLA Modules:
  0.0 141.7 jit_solution(16007888642769260608)
XLA Ops:
  6.3 4.0 %collective-permute-start.2 = (f32[128,1024]{1,0:T(8,128)}, f32[128,1024]{1,0:T(8,128)}, u32[]{:S(2)}, u32[]{:S(2)}) collective-permute-start(f32[128,1024]{1,0:T(8,128)} %choose.1), channel_id=1, source_target_pairs={{0,16},{1,17},{2,18},{3,19},{4,20},{5,21},{6,22},{7,23},{8,24},{9,... | collective-permute-start | bytes 1572872 | tf_op jit(solution)/shard_map/ppermute | solution.py:45
  13.6 2.2 %copy-done.4 = f32[1024,1024]{1,0:T(8,128)S(1)} copy-done((f32[1024,1024]{1,0:T(8,128)S(1)}, f32[1024,1024]{1,0:T(8,128)}, u32[]{:S(2)}) %copy-start.4) | copy-done | bytes 4194328
  15.8 5.5 %project.1 = (f32[256,1024]{1,0:T(8,128)}, f32[256,1024]{1,0:T(8,128)}) custom-call(s32[9]{0:T(128)S(1)} %stack.43.place_ref, f32[256,1024]{1,0:T(8,128)S(1)} %copy-done.3, f32[256,1024]{1,0:T(8,128)S(1)} %copy-done.1, f32[1024,1024]{1,0:T(8,128)S(1)} %copy-done.4), custom_call_target="tpu_custom_call" | custom-call | flops 1 | bytes 1 | tf_op jit(solution)/shard_map/project/pallas_call | solution.py:24
  25.0 14.5 %collective-permute-done.3.far_ref = f32[128,256]{1,0:T(8,128)S(1)} collective-permute-done((f32[128,256]{1,0:T(8,128)}, f32[128,256]{1,0:T(8,128)S(1)}, u32[]{:S(2)}, u32[]{:S(2)}) %collective-permute-start.3) | collective-permute-done | bytes 131104 | tf_op jit(solution)/shard_map/ppermute | solution.py:45
  39.5 2.1 %collective-permute-done.4.other_ref = f32[128,1024]{1,0:T(8,128)S(1)} collective-permute-done((f32[128,1024]{1,0:T(8,128)}, f32[128,1024]{1,0:T(8,128)S(1)}, u32[]{:S(2)}, u32[]{:S(2)}) %collective-permute-start.4) | collective-permute-done | bytes 524320 | tf_op jit(solution)/shard_map/ppermute | solution.py:45
  44.3 2.1 %collective-permute-start.7 = (f32[64,1024]{1,0:T(8,128)S(1)}, f32[64,1024]{1,0:T(8,128)S(1)}, u32[]{:S(2)}, u32[]{:S(2)}) collective-permute-start(f32[64,1024]{1,0:T(8,128)S(1)} %get-tuple-element.151), channel_id=1, source_target_pairs={{0,8},{1,9},{2,10},{3,11},{4,12},{5,13},{6,14},{7,15},{8,0},{9,1},... | collective-permute-start | bytes 786440 | tf_op jit(solution)/shard_map/ppermute | solution.py:45
  46.4 3.1 %collective-permute-done.5.far_ref = f32[128,256]{1,0:T(8,128)S(1)} collective-permute-done((f32[128,256]{1,0:T(8,128)}, f32[128,256]{1,0:T(8,128)S(1)}, u32[]{:S(2)}, u32[]{:S(2)}) %collective-permute-start.5) | collective-permute-done | bytes 131104 | tf_op jit(solution)/shard_map/ppermute | solution.py:45
  52.5 5.4 %collective-permute-done.7.received_ref = f32[64,1024]{1,0:T(8,128)S(1)} collective-permute-done((f32[64,1024]{1,0:T(8,128)S(1)}, f32[64,1024]{1,0:T(8,128)S(1)}, u32[]{:S(2)}, u32[]{:S(2)}) %collective-permute-start.7) | collective-permute-done | bytes 262176 | tf_op jit(solution)/shard_map/ppermute | solution.py:45
  62.2 2.7 %collective-permute-start.12 = (f32[64,1024]{1,0:T(8,128)S(1)}, f32[64,1024]{1,0:T(8,128)S(1)}, u32[]{:S(2)}, u32[]{:S(2)}) collective-permute-start(f32[64,1024]{1,0:T(8,128)S(1)} %get-tuple-element.173), channel_id=1, source_target_pairs={{0,8},{1,9},{2,10},{3,11},{4,12},{5,13},{6,14},{7,15},{8,0},{9,1},... | collective-permute-start | bytes 786440 | tf_op jit(solution)/shard_map/ppermute | solution.py:45
  70.2 2.2 %collective-permute-start.14 = (f32[32,1024]{1,0:T(8,128)S(1)}, f32[32,1024]{1,0:T(8,128)S(1)}, u32[]{:S(2)}, u32[]{:S(2)}) collective-permute-start(f32[32,1024]{1,0:T(8,128)S(1)} %copy-done.5), channel_id=1, source_target_pairs={{0,16},{1,17},{2,18},{3,19},{4,20},{5,21},{6,22},{7,23},{8,24},{9,... | collective-permute-start | bytes 393224 | tf_op jit(solution)/shard_map/ppermute | solution.py:45
  72.4 2.2 %collective-permute-done.18.far_ref = f32[128,256]{1,0:T(8,128)S(1)} collective-permute-done((f32[128,256]{1,0:T(8,128)S(1)}, f32[128,256]{1,0:T(8,128)S(1)}, u32[]{:S(2)}, u32[]{:S(2)}) %collective-permute-start.18) | collective-permute-done | bytes 131104 | tf_op jit(solution)/shard_map/ppermute | solution.py:45
  75.9 3.0 %collective-permute-start.19 = (f32[64,1024]{1,0:T(8,128)S(1)}, f32[64,1024]{1,0:T(8,128)S(1)}, u32[]{:S(2)}, u32[]{:S(2)}) collective-permute-start(f32[64,1024]{1,0:T(8,128)S(1)} %get-tuple-element.197), channel_id=1, source_target_pairs={{0,8},{1,9},{2,10},{3,11},{4,12},{5,13},{6,14},{7,15},{8,0},{9,1},... | collective-permute-start | bytes 786440 | tf_op jit(solution)/shard_map/ppermute | solution.py:45
  80.1 2.4 %collective-permute-start.13 = (f32[16,1024]{1,0:T(8,128)S(1)}, f32[16,1024]{1,0:T(8,128)S(1)}, u32[]{:S(2)}, u32[]{:S(2)}) collective-permute-start(f32[16,1024]{1,0:T(8,128)S(1)} %merge.4.kept_ref), channel_id=1, source_target_pairs={{0,16},{1,17},{2,18},{3,19},{4,20},{5,21},{6,22},{7,23},{8,24},{9,... | collective-permute-start | bytes 196616 | tf_op jit(solution)/shard_map/ppermute | solution.py:45
  88.5 2.3 %collective-permute-start.20 = (f32[16,1024]{1,0:T(8,128)S(1)}, f32[16,1024]{1,0:T(8,128)S(1)}, u32[]{:S(2)}, u32[]{:S(2)}) collective-permute-start(f32[16,1024]{1,0:T(8,128)S(1)} %merge.5.kept_ref), channel_id=1, source_target_pairs={{0,16},{1,17},{2,18},{3,19},{4,20},{5,21},{6,22},{7,23},{8,24},{9,... | collective-permute-start | bytes 196616 | tf_op jit(solution)/shard_map/ppermute | solution.py:45
  96.1 2.2 %collective-permute-start.28 = (f32[32,1024]{1,0:T(8,128)S(1)}, f32[32,1024]{1,0:T(8,128)S(1)}, u32[]{:S(2)}, u32[]{:S(2)}) collective-permute-start(f32[32,1024]{1,0:T(8,128)S(1)} %constant_dynamic-update-slice_fusion.refs_0_), channel_id=1, source_target_pairs={{0,8},{1,9},{2,10},{3,11},{4,12},{5,13},{6,14},{7,15},{8,0},{9,1},... | collective-permute-start | bytes 393224 | tf_op jit(solution)/shard_map/ppermute | solution.py:45
  99.9 2.0 %collective-permute-start.24 = (f32[32,1024]{1,0:T(8,128)S(1)}, f32[32,1024]{1,0:T(8,128)S(1)}, u32[]{:S(2)}, u32[]{:S(2)}) collective-permute-start(f32[32,1024]{1,0:T(8,128)S(1)} %constant_dynamic-update-slice_fusion.refs_0_), channel_id=1, source_target_pairs={{0,4},{1,5},{2,6},{3,7},{4,0},{5,1},{6,2},{7,3},{8,12},{9,13},{10,... | collective-permute-start | bytes 393224 | tf_op jit(solution)/shard_map/ppermute | solution.py:45
  102.7 2.0 %collective-permute-start.22 = (f32[32,1024]{1,0:T(8,128)S(1)}, f32[32,1024]{1,0:T(8,128)S(1)}, u32[]{:S(2)}, u32[]{:S(2)}) collective-permute-start(f32[32,1024]{1,0:T(8,128)S(1)} %constant_dynamic-update-slice_fusion.refs_0_), channel_id=1, source_target_pairs={{0,2},{1,3},{2,0},{3,1},{4,6},{5,7},{6,4},{7,5},{8,10},{9,11},{10,... | collective-permute-start | bytes 393224 | tf_op jit(solution)/shard_map/ppermute | solution.py:45
  110.9 2.3 %collective-permute-done.40.received_ref = f32[16,1024]{1,0:T(8,128)S(1)} collective-permute-done((f32[16,1024]{1,0:T(8,128)S(1)}, f32[16,1024]{1,0:T(8,128)S(1)}, u32[]{:S(2)}, u32[]{:S(2)}) %collective-permute-start.40) | collective-permute-done | bytes 65568 | tf_op jit(solution)/shard_map/ppermute | solution.py:45
  125.2 2.6 %collective-permute-start.52 = (f32[32,1024]{1,0:T(8,128)S(1)}, f32[32,1024]{1,0:T(8,128)S(1)}, u32[]{:S(2)}, u32[]{:S(2)}) collective-permute-start(f32[32,1024]{1,0:T(8,128)S(1)} %collective-permute-done.44.refs_20_), channel_id=1, source_target_pairs={{0,8},{1,9},{2,10},{3,11},{4,12},{5,13},{6,14},{7,15},{8,0},{9,1},... | collective-permute-start | bytes 393224 | tf_op jit(solution)/shard_map/ppermute | solution.py:45
  128.0 2.0 %collective-permute-start.54 = (f32[32,1024]{1,0:T(8,128)S(1)}, f32[32,1024]{1,0:T(8,128)S(1)}, u32[]{:S(2)}, u32[]{:S(2)}) collective-permute-start(f32[32,1024]{1,0:T(8,128)S(1)} %collective-permute-done.46.refs_22_), channel_id=1, source_target_pairs={{0,8},{1,9},{2,10},{3,11},{4,12},{5,13},{6,14},{7,15},{8,0},{9,1},... | collective-permute-start | bytes 393224 | tf_op jit(solution)/shard_map/ppermute | solution.py:45
  130.0 1.8 %collective-permute-done.52.refs_28_ = f32[32,1024]{1,0:T(8,128)S(1)} collective-permute-done((f32[32,1024]{1,0:T(8,128)S(1)}, f32[32,1024]{1,0:T(8,128)S(1)}, u32[]{:S(2)}, u32[]{:S(2)}) %collective-permute-start.52) | collective-permute-done | bytes 131104 | tf_op jit(solution)/shard_map/ppermute | solution.py:45
  132.3 2.1 %collective-permute-done.50.refs_26_ = f32[32,1024]{1,0:T(8,128)S(1)} collective-permute-done((f32[32,1024]{1,0:T(8,128)S(1)}, f32[32,1024]{1,0:T(8,128)S(1)}, u32[]{:S(2)}, u32[]{:S(2)}) %collective-permute-start.50) | collective-permute-done | bytes 131104 | tf_op jit(solution)/shard_map/ppermute | solution.py:45
  134.4 2.3 %collective-permute-done.54.refs_30_ = f32[32,1024]{1,0:T(8,128)S(1)} collective-permute-done((f32[32,1024]{1,0:T(8,128)S(1)}, f32[32,1024]{1,0:T(8,128)S(1)}, u32[]{:S(2)}, u32[]{:S(2)}) %collective-permute-start.54) | collective-permute-done | bytes 131104 | tf_op jit(solution)/shard_map/ppermute | solution.py:45
  138.0 3.6 %finish.1 = (f32[1024,1024]{1,0:T(8,128)}, f32[256,1024]{1,0:T(8,128)}) custom-call(s32[9]{0:T(128)S(1)} %stack.43.place_ref, f32[256,1024]{1,0:T(8,128)S(1)} %copy-done.3, f32[32,1024]{1,0:T(8,128)S(1)} %constant_dynamic-update-slice_fusion.refs_0_, f32[32,1024]{1,0:T(8,128)S(1)} %collective-permute-done.21.refs_1_, ...), custom_call_target="tpu_custom_call" | custom-call | flops 1 | bytes 1 | tf_op jit(solution)/shard_map/finish/pallas_call | solution.py:24
  (148 shorter events, 64.1 us)
Async XLA Ops:
  3.4 6.9 %collective-permute-start = (f32[512,256]{1,0:T(8,128)S(1)}, f32[512,256]{1,0:T(8,128)S(1)}, u32[]{:S(2)}, u32[]{:S(2)}) collective-permute-start(f32[512,256]{1,0:T(8,128)S(1)} %get-tuple-element.119), channel_id=1, source_target_pairs={{0,1},{1,0},{2,3},{3,2},{4,5},{5,4},{6,7},{7,6},{8,9},{9,8},{10,11... | collective-permute-start | bytes 1572872 | tf_op jit(solution)/shard_map/ppermute | solution.py:45
  6.3 33.2 %collective-permute-start.2 = (f32[128,1024]{1,0:T(8,128)}, f32[128,1024]{1,0:T(8,128)}, u32[]{:S(2)}, u32[]{:S(2)}) collective-permute-start(f32[128,1024]{1,0:T(8,128)} %choose.1), channel_id=1, source_target_pairs={{0,16},{1,17},{2,18},{3,19},{4,20},{5,21},{6,22},{7,23},{8,24},{9,... | collective-permute-start | bytes 1572872 | tf_op jit(solution)/shard_map/ppermute | solution.py:45
  13.6 25.9 %collective-permute-start.3 = (f32[128,256]{1,0:T(8,128)}, f32[128,256]{1,0:T(8,128)S(1)}, u32[]{:S(2)}, u32[]{:S(2)}) collective-permute-start(f32[128,256]{1,0:T(8,128)} %get-tuple-element.127), channel_id=1, source_target_pairs={{0,16},{1,17},{2,18},{3,19},{4,20},{5,21},{6,22},{7,23},{8,24},{9,... | collective-permute-start | bytes 393224 | tf_op jit(solution)/shard_map/ppermute | solution.py:45
  39.5 9.9 %collective-permute-start.5 = (f32[128,256]{1,0:T(8,128)}, f32[128,256]{1,0:T(8,128)S(1)}, u32[]{:S(2)}, u32[]{:S(2)}) collective-permute-start(f32[128,256]{1,0:T(8,128)} %copy-done.12), channel_id=1, source_target_pairs={{0,16},{1,17},{2,18},{3,19},{4,20},{5,21},{6,22},{7,23},{8,24},{9,... | collective-permute-start | bytes 393224 | tf_op jit(solution)/shard_map/ppermute | solution.py:45
  44.3 13.6 %collective-permute-start.7 = (f32[64,1024]{1,0:T(8,128)S(1)}, f32[64,1024]{1,0:T(8,128)S(1)}, u32[]{:S(2)}, u32[]{:S(2)}) collective-permute-start(f32[64,1024]{1,0:T(8,128)S(1)} %get-tuple-element.151), channel_id=1, source_target_pairs={{0,8},{1,9},{2,10},{3,11},{4,12},{5,13},{6,14},{7,15},{8,0},{9,1},... | collective-permute-start | bytes 786440 | tf_op jit(solution)/shard_map/ppermute | solution.py:45
  50.8 14.8 %collective-permute-start.6 = (f32[64,1024]{1,0:T(8,128)S(1)}, f32[64,1024]{1,0:T(8,128)S(1)}, u32[]{:S(2)}, u32[]{:S(2)}) collective-permute-start(f32[64,1024]{1,0:T(8,128)S(1)} %get-tuple-element.140), channel_id=1, source_target_pairs={{0,8},{1,9},{2,10},{3,11},{4,12},{5,13},{6,14},{7,15},{8,0},{9,1},... | collective-permute-start | bytes 786440 | tf_op jit(solution)/shard_map/ppermute | solution.py:45
  50.9 9.9 %collective-permute-start.11 = (f32[128,256]{1,0:T(8,128)}, f32[128,256]{1,0:T(8,128)S(1)}, u32[]{:S(2)}, u32[]{:S(2)}) collective-permute-start(f32[128,256]{1,0:T(8,128)} %copy-done.11), channel_id=1, source_target_pairs={{0,16},{1,17},{2,18},{3,19},{4,20},{5,21},{6,22},{7,23},{8,24},{9,... | collective-permute-start | bytes 393224 | tf_op jit(solution)/shard_map/ppermute | solution.py:45
  58.6 7.0 %collective-permute-start.8 = (f32[32,1024]{1,0:T(8,128)S(1)}, f32[32,1024]{1,0:T(8,128)S(1)}, u32[]{:S(2)}, u32[]{:S(2)}) collective-permute-start(f32[32,1024]{1,0:T(8,128)S(1)} %get-tuple-element.155), channel_id=1, source_target_pairs={{0,4},{1,5},{2,6},{3,7},{4,0},{5,1},{6,2},{7,3},{8,12},{9,13},{10,... | collective-permute-start | bytes 393224 | tf_op jit(solution)/shard_map/ppermute | solution.py:45
  62.2 21.0 %collective-permute-start.12 = (f32[64,1024]{1,0:T(8,128)S(1)}, f32[64,1024]{1,0:T(8,128)S(1)}, u32[]{:S(2)}, u32[]{:S(2)}) collective-permute-start(f32[64,1024]{1,0:T(8,128)S(1)} %get-tuple-element.173), channel_id=1, source_target_pairs={{0,8},{1,9},{2,10},{3,11},{4,12},{5,13},{6,14},{7,15},{8,0},{9,1},... | collective-permute-start | bytes 786440 | tf_op jit(solution)/shard_map/ppermute | solution.py:45
  64.9 9.6 %collective-permute-start.18 = (f32[128,256]{1,0:T(8,128)S(1)}, f32[128,256]{1,0:T(8,128)S(1)}, u32[]{:S(2)}, u32[]{:S(2)}) collective-permute-start(f32[128,256]{1,0:T(8,128)S(1)} %copy-done.10), channel_id=1, source_target_pairs={{0,16},{1,17},{2,18},{3,19},{4,20},{5,21},{6,22},{7,23},{8,24},{9,... | collective-permute-start | bytes 393224 | tf_op jit(solution)/shard_map/ppermute | solution.py:45
  66.3 12.6 %collective-permute-start.9 = (f32[16,1024]{1,0:T(8,128)S(1)}, f32[16,1024]{1,0:T(8,128)S(1)}, u32[]{:S(2)}, u32[]{:S(2)}) collective-permute-start(f32[16,1024]{1,0:T(8,128)S(1)} %get-tuple-element.159), channel_id=1, source_target_pairs={{0,2},{1,3},{2,0},{3,1},{4,6},{5,7},{6,4},{7,5},{8,10},{9,11},{10,... | collective-permute-start | bytes 196616 | tf_op jit(solution)/shard_map/ppermute | solution.py:45
  68.6 11.6 %collective-permute-start.10 = (f32[32,1024]{1,0:T(8,128)S(1)}, f32[32,1024]{1,0:T(8,128)S(1)}, u32[]{:S(2)}, u32[]{:S(2)}) collective-permute-start(f32[32,1024]{1,0:T(8,128)S(1)} %get-tuple-element.162), channel_id=1, source_target_pairs={{0,4},{1,5},{2,6},{3,7},{4,0},{5,1},{6,2},{7,3},{8,12},{9,13},{10,... | collective-permute-start | bytes 393224 | tf_op jit(solution)/shard_map/ppermute | solution.py:45
  70.2 15.3 %collective-permute-start.14 = (f32[32,1024]{1,0:T(8,128)S(1)}, f32[32,1024]{1,0:T(8,128)S(1)}, u32[]{:S(2)}, u32[]{:S(2)}) collective-permute-start(f32[32,1024]{1,0:T(8,128)S(1)} %copy-done.5), channel_id=1, source_target_pairs={{0,16},{1,17},{2,18},{3,19},{4,20},{5,21},{6,22},{7,23},{8,24},{9,... | collective-permute-start | bytes 393224 | tf_op jit(solution)/shard_map/ppermute | solution.py:45
  75.9 17.1 %collective-permute-start.19 = (f32[64,1024]{1,0:T(8,128)S(1)}, f32[64,1024]{1,0:T(8,128)S(1)}, u32[]{:S(2)}, u32[]{:S(2)}) collective-permute-start(f32[64,1024]{1,0:T(8,128)S(1)} %get-tuple-element.197), channel_id=1, source_target_pairs={{0,8},{1,9},{2,10},{3,11},{4,12},{5,13},{6,14},{7,15},{8,0},{9,1},... | collective-permute-start | bytes 786440 | tf_op jit(solution)/shard_map/ppermute | solution.py:45
  78.9 8.2 %collective-permute-start.15 = (f32[32,1024]{1,0:T(8,128)S(1)}, f32[32,1024]{1,0:T(8,128)S(1)}, u32[]{:S(2)}, u32[]{:S(2)}) collective-permute-start(f32[32,1024]{1,0:T(8,128)S(1)} %copy-done.6), channel_id=1, source_target_pairs={{0,16},{1,17},{2,18},{3,19},{4,20},{5,21},{6,22},{7,23},{8,24},{9,... | collective-permute-start | bytes 393224 | tf_op jit(solution)/shard_map/ppermute | solution.py:45
  80.1 6.9 %collective-permute-start.13 = (f32[16,1024]{1,0:T(8,128)S(1)}, f32[16,1024]{1,0:T(8,128)S(1)}, u32[]{:S(2)}, u32[]{:S(2)}) collective-permute-start(f32[16,1024]{1,0:T(8,128)S(1)} %merge.4.kept_ref), channel_id=1, source_target_pairs={{0,16},{1,17},{2,18},{3,19},{4,20},{5,21},{6,22},{7,23},{8,24},{9,... | collective-permute-start | bytes 196616 | tf_op jit(solution)/shard_map/ppermute | solution.py:45
  91.5 6.7 %collective-permute-start.36 = (f32[16,1024]{1,0:T(8,128)S(1)}, f32[16,1024]{1,0:T(8,128)S(1)}, u32[]{:S(2)}, u32[]{:S(2)}) collective-permute-start(f32[16,1024]{1,0:T(8,128)S(1)} %get-tuple-element.204), channel_id=1, source_target_pairs={{0,2},{1,3},{2,0},{3,1},{4,6},{5,7},{6,4},{7,5},{8,10},{9,11},{10,... | collective-permute-start | bytes 196616 | tf_op jit(solution)/shard_map/ppermute | solution.py:45
  93.8 8.2 %collective-permute-start.37 = (f32[32,1024]{1,0:T(8,128)S(1)}, f32[32,1024]{1,0:T(8,128)S(1)}, u32[]{:S(2)}, u32[]{:S(2)}) collective-permute-start(f32[32,1024]{1,0:T(8,128)S(1)} %get-tuple-element.207), channel_id=1, source_target_pairs={{0,4},{1,5},{2,6},{3,7},{4,0},{5,1},{6,2},{7,3},{8,12},{9,13},{10,... | collective-permute-start | bytes 393224 | tf_op jit(solution)/shard_map/ppermute | solution.py:45
  96.1 8.6 %collective-permute-start.28 = (f32[32,1024]{1,0:T(8,128)S(1)}, f32[32,1024]{1,0:T(8,128)S(1)}, u32[]{:S(2)}, u32[]{:S(2)}) collective-permute-start(f32[32,1024]{1,0:T(8,128)S(1)} %constant_dynamic-update-slice_fusion.refs_0_), channel_id=1, source_target_pairs={{0,8},{1,9},{2,10},{3,11},{4,12},{5,13},{6,14},{7,15},{8,0},{9,1},... | collective-permute-start | bytes 393224 | tf_op jit(solution)/shard_map/ppermute | solution.py:45
  99.9 8.7 %collective-permute-start.24 = (f32[32,1024]{1,0:T(8,128)S(1)}, f32[32,1024]{1,0:T(8,128)S(1)}, u32[]{:S(2)}, u32[]{:S(2)}) collective-permute-start(f32[32,1024]{1,0:T(8,128)S(1)} %constant_dynamic-update-slice_fusion.refs_0_), channel_id=1, source_target_pairs={{0,4},{1,5},{2,6},{3,7},{4,0},{5,1},{6,2},{7,3},{8,12},{9,13},{10,... | collective-permute-start | bytes 393224 | tf_op jit(solution)/shard_map/ppermute | solution.py:45
  102.7 7.4 %collective-permute-start.22 = (f32[32,1024]{1,0:T(8,128)S(1)}, f32[32,1024]{1,0:T(8,128)S(1)}, u32[]{:S(2)}, u32[]{:S(2)}) collective-permute-start(f32[32,1024]{1,0:T(8,128)S(1)} %constant_dynamic-update-slice_fusion.refs_0_), channel_id=1, source_target_pairs={{0,2},{1,3},{2,0},{3,1},{4,6},{5,7},{6,4},{7,5},{8,10},{9,11},{10,... | collective-permute-start | bytes 393224 | tf_op jit(solution)/shard_map/ppermute | solution.py:45
  110.1 6.7 %collective-permute-start.26 = (f32[32,1024]{1,0:T(8,128)S(1)}, f32[32,1024]{1,0:T(8,128)S(1)}, u32[]{:S(2)}, u32[]{:S(2)}) collective-permute-start(f32[32,1024]{1,0:T(8,128)S(1)} %collective-permute-done.24.refs_4_), channel_id=1, source_target_pairs={{0,2},{1,3},{2,0},{3,1},{4,6},{5,7},{6,4},{7,5},{8,10},{9,11},{10,... | collective-permute-start | bytes 393224 | tf_op jit(solution)/shard_map/ppermute | solution.py:45
  128.0 8.7 %collective-permute-start.54 = (f32[32,1024]{1,0:T(8,128)S(1)}, f32[32,1024]{1,0:T(8,128)S(1)}, u32[]{:S(2)}, u32[]{:S(2)}) collective-permute-start(f32[32,1024]{1,0:T(8,128)S(1)} %collective-permute-done.46.refs_22_), channel_id=1, source_target_pairs={{0,8},{1,9},{2,10},{3,11},{4,12},{5,13},{6,14},{7,15},{8,0},{9,1},... | collective-permute-start | bytes 393224 | tf_op jit(solution)/shard_map/ppermute | solution.py:45
  130.0 7.4 %collective-permute-start.43 = (f32[32,1024]{1,0:T(8,128)S(1)}, f32[32,1024]{1,0:T(8,128)S(1)}, u32[]{:S(2)}, u32[]{:S(2)}) collective-permute-start(f32[32,1024]{1,0:T(8,128)S(1)} %collective-permute-done.42.refs_18_), channel_id=1, source_target_pairs={{0,1},{1,0},{2,3},{3,2},{4,5},{5,4},{6,7},{7,6},{8,9},{9,8},{10,11... | collective-permute-start | bytes 393224 | tf_op jit(solution)/shard_map/ppermute | solution.py:45
  (45 other events, 319.6 us)

commit v2 on v1

v2 whole, which is shorter than its diff:
```python
import functools
import jax
import jax.numpy as jnp
from jax import lax
from jax.experimental import pallas as pl
from jax.experimental.pallas import tpu as pltpu
from jax.sharding import PartitionSpec as P

beta_one = 0.9
beta_two = 0.999
rate_value = 0.01
step_count = 10
adam_epsilon = 1e-08
norm_epsilon = 1e-06

MESSAGES = [[0], [1, 2, 3]]
GROUPS = [[0, 1], [2, 3]]
ORDER = [(0, 1), (1, 1), (0, 2), (1, 2), (0, 3), (1, 3), (0, 4), (1, 4)]
AHEAD = 1
JOIN, FRESH, DIRECT = True,False,0


OWNER, TOP, MIDDLE, CORE, BITS = range(5)


def kernel_call(kernel, name, outs, megabytes, place, *arrays, after=()):
    vmem = pl.BlockSpec(memory_space=pltpu.VMEM)
    count = 1 + len(arrays)

    def body(*refs):
        kernel(*refs[:count], *refs[count + len(after) :])

    return pl.pallas_call(
        body,
        out_shape=tuple(outs),
        in_specs=[pl.BlockSpec(memory_space=pltpu.SMEM)]
        + [vmem] * len(arrays)
        + [pl.BlockSpec(memory_space=pl.ANY)] * len(after),
        out_specs=tuple(vmem for _ in outs),
        compiler_params=pltpu.CompilerParams(vmem_limit_bytes=megabytes << 20),
        cost_estimate=pl.CostEstimate(flops=1, bytes_accessed=1, transcendentals=0),
        name=name,
    )(place, *arrays, *after)


def f32(*shape):
    return jax.ShapeDtypeStruct(shape, jnp.float32)


def bf16(*shape):
    return jax.ShapeDtypeStruct(shape, jnp.bfloat16)


def swapped(block, mask, owners=None):
    count = lax.axis_size("dp")
    high = count.bit_length() - 2
    return lax.ppermute(
        block, "dp", [(i, i ^ mask) for i in range(count) if owners is None or ((i & 1) == i >> high) == owners]
    )


def parts(x):
    high = x.astype(jnp.bfloat16)
    return high, (x - high.astype(jnp.float32)).astype(jnp.bfloat16)


def product(left, right, contract=0):
    left_high, left_low = left
    right_high, right_low = right

    def dot(a, b):
        return lax.dot_general(
            a, b, (((1,), (contract,)), ((), ())), preferred_element_type=jnp.float32
        )

    return dot(left_high, right_high) + (dot(left_high, right_low) + dot(left_low, right_high))


def combine(left_rows, right_rows):
    cross_term = jnp.sum(left_rows * right_rows, axis=-1, keepdims=True)
    left_norm = jnp.sum(left_rows * left_rows, axis=-1, keepdims=True)
    right_norm = jnp.sum(right_rows * right_rows, axis=-1, keepdims=True)
    left_coef = 1.0 - cross_term / (2.0 * (left_norm + norm_epsilon))
    right_coef = 1.0 - cross_term / (2.0 * (right_norm + norm_epsilon))
    return left_coef * left_rows + right_coef * right_rows


def adam_update(gradient, weight_rows, first_rows, second_rows):
    first_new = beta_one * first_rows + (1.0 - beta_one) * gradient
    second_new = beta_two * second_rows + (1.0 - beta_two) * gradient * gradient
    first_hat = first_new / (1.0 - beta_one**step_count)
    second_hat = second_new / (1.0 - beta_two**step_count)
    weight_new = weight_rows - rate_value * first_hat / (jnp.sqrt(second_hat) + adam_epsilon)
    return (weight_new, first_new, second_new)


def prepare_kernel(middle, own, spans, place_ref, tokens_ref, keep_ref, other_ref):
    def fill(mine):
        width = 128
        for base in range(0, tokens_ref.shape[1], width):
            block = tokens_ref[:, base : base + width].T
            for group in range(base // own, (base + width) // own):
                node, here = divmod(group, 2)
                top, mid = divmod(node, middle)
                target = keep_ref if here == mine else other_ref
                for first, piece in spans:
                    row = first * middle * 2 + (mid * 2 + top) * piece
                    low = group * own + first - base
                    target[row : row + piece, :] = block[low : low + piece, :]

    for mine in range(2):
        pl.when(place_ref[CORE] == mine)(functools.partial(fill, mine))


def choose_kernel(place_ref, cotangent_ref, swap_ref, send_ref):
    half = send_ref.shape[0]
    send_ref[...] = jnp.where(place_ref[OWNER] == 1, swap_ref[half:, :], cotangent_ref[:half, :])


def share_kernel(place_ref, keep_ref, swap_ref, near_ref, *send_refs):
    owner = place_ref[OWNER] == 1
    near_ref[...] = jnp.where(owner, keep_ref[...], swap_ref[...])
    row = 0
    for send_ref in send_refs:
        rows = slice(row, row + send_ref.shape[0])
        send_ref[...] = jnp.where(owner, swap_ref[rows, :], keep_ref[rows, :])
        row += send_ref.shape[0]


def project_kernel(place_ref, tokens_ref, cotangent_ref, weight_ref, projected_ref, grad_ref):
    tokens = parts(tokens_ref[...])
    cotangent = parts(cotangent_ref[...])
    width = weight_ref.shape[0]
    step = min(256, width)
    for base in range(0, width, step):
        span = slice(base, base + step)
        projected_ref[:, span] = product(tokens, parts(weight_ref[:, span]))
        grad_ref[:, span] = product(cotangent, parts(weight_ref[span, :]), 1)


def near_kernel(scale, place_ref, tokens_ref, cotangent_ref, swap_ref, near_ref):
    right = parts(jnp.where(place_ref[OWNER] == 1, cotangent_ref[...], swap_ref[...]))
    near_ref[...] = product(parts(tokens_ref[...]), right) * scale


def assemble_kernel(place_ref, mine_ref, other_ref, high_ref, low_ref):
    owner = place_ref[OWNER] == 1
    half = mine_ref.shape[0]
    for at in range(2):
        rows = slice(at * half, (at + 1) * half)
        chosen = jnp.where(owner == (at == 0), mine_ref[...], other_ref[...])
        high_ref[rows, :], low_ref[rows, :] = parts(chosen)


def halves(place_ref, bit, start, half):
    mine = place_ref[BITS + bit]
    return [(start, part, half) for part in (mine, 1 - mine)]


def taken(ref, rows):
    start, part, half = rows
    if half % 8 == 0:
        return ref[pl.ds(pl.multiple_of(start + part * half, half), half), :]
    return jnp.where(part == 1, ref[start + half : start + 2 * half, :], ref[start : start + half, :])


def first_kernel(scale, bit, near_start, far_start, place_ref, near_ref, far_ref, high_ref, low_ref, keep_ref, send_ref):
    right = (high_ref[...], low_ref[...])
    half = keep_ref.shape[0]
    near_rows = halves(place_ref, bit, near_start, half)
    far_rows = halves(place_ref, bit, far_start, half)
    for target, at in ((send_ref, 1), (keep_ref, 0)):
        far = product(parts(taken(far_ref, far_rows[at])), right) * scale
        target[...] = combine(taken(near_ref, near_rows[at]), far)


def middle_kernel(bit, segment, place_ref, *refs):
    *pairs, keep_ref, send_ref = refs
    half = segment // 2
    out = 0
    for kept_ref, received_ref in zip(pairs[::2], pairs[1::2]):
        for start in range(0, kept_ref.shape[0], segment):
            for target, rows in zip((keep_ref, send_ref), halves(place_ref, bit, start, half)):
                target[out : out + half, :] = combine(taken(kept_ref, rows), taken(received_ref, rows))
            out += half


def last_kernel(
    spans, place_ref, kept_ref, received_ref, weight_ref, first_ref, second_ref,
    weight_out, first_out, second_out,
):
    first, rows = spans[0][0], kept_ref.shape[0]
    span = slice(first, first + rows)
    weight_out[...], first_out[...], second_out[...] = adam_update(
        combine(kept_ref[...], received_ref[...]), weight_ref[span, :], first_ref[span, :], second_ref[span, :]
    )


def pair_kernel(place_ref, *refs):
    *row_refs, out_ref = refs
    half = out_ref.shape[0] // 2
    count = len(row_refs) // 2
    top = place_ref[TOP]
    for side, group in ((top, row_refs[:count]), (1 - top, row_refs[count:])):
        start = 0
        for row_ref in group:
            rows = row_ref.shape[0]
            out_ref[pl.ds(pl.multiple_of(side * half + start, rows), rows), :] = row_ref[...]
            start += rows


def finish_kernel(middle, own, streams, place_ref, tokens_ref, *refs):
    *block_refs, weight_ref, projected_ref = refs
    mid, core = place_ref[MIDDLE], place_ref[CORE]
    for at, block_ref in enumerate(block_refs):
        stream, at = divmod(at, 2 * middle)
        far_mid, far_core = divmod(at, 2)
        device = (mid ^ far_mid) * 2 + (core ^ far_core)
        first, rows = streams[stream][0][0], block_ref.shape[0] // 2
        for top in range(2):
            row = (device + top * middle * 2) * own + first
            weight_ref[pl.ds(pl.multiple_of(row, 8), rows), :] = block_ref[top * rows : (top + 1) * rows, :]
    depth = min(256, tokens_ref.shape[1])
    total = jnp.zeros(projected_ref.shape, jnp.float32)
    for base in range(0, tokens_ref.shape[1], depth):
        span = slice(base, base + depth)
        total = total + product(parts(tokens_ref[:, span]), parts(weight_ref[span, :]))
    projected_ref[...] = total


def relative_blocks(rows, bits, load, direct):
    blocks = {0: rows}
    masks = [sum(1 << bits[at] for at in range(len(bits)) if pick >> at & 1) for pick in range(1, 1 << len(bits))]
    for mask in sorted(masks, key=lambda mask: mask.bit_count()):
        inside = [bit for bit in bits if mask >> bit & 1]
        if direct and len(inside) > 2:
            blocks[mask] = swapped(rows, mask)
            continue
        if mask.bit_count() == 2 and len(bits) == 3:
            at = bits.index(inside[0])
            last = inside[1] if bits[(at + 1) % 3] == inside[1] else inside[0]
        else:
            last = min(inside, key=lambda bit: load[bit])
        load[last] += 1
        blocks[mask] = swapped(blocks[mask ^ 1 << last], 1 << last)
    return blocks


def on_device(tokens, cotangent, weight, first_moment, second_moment):
    token_count, width = tokens.shape
    devices = lax.axis_size("dp")
    levels = devices.bit_length() - 1
    index = lax.axis_index("dp")
    own = width // devices
    middle = devices // 4
    units = 4 if own % 32 == 0 else 1
    piece = own // units
    spans = [(at * piece, piece) for at in range(units)]
    messages = MESSAGES if units == 4 else [[0]]
    groups = GROUPS if units == 4 else [[0]]
    streams = [[spans[unit] for unit in group] for group in groups]
    top_mask = devices >> 1
    core, top = index & 1, index >> levels - 1
    scale = 1.0 / token_count
    place = jnp.stack(
        [(core == top).astype(jnp.int32), top, index >> 1 & middle - 1, core]
        + [index >> bit & 1 for bit in range(levels)]
    )
    half_rows = width // 2

    cotangent_swap = swapped(cotangent, 1)
    tokens_keep, tokens_other = kernel_call(
        functools.partial(prepare_kernel, middle, own, spans), "prepare",
        [f32(half_rows, token_count)] * 2, 4, place, tokens,
    )
    tokens_swap = swapped(tokens_other, 1)
    (send_cotangent,) = kernel_call(
        choose_kernel, "choose", [f32(token_count // 2, width)], 4, place, cotangent, cotangent_swap
    )
    far_mine = swapped(send_cotangent, top_mask)
    unit_rows = half_rows // units
    near_tokens, *send_tokens = kernel_call(
        share_kernel, "share",
        [f32(half_rows, token_count)] + [f32(unit_rows * len(message), token_count) for message in messages],
        4, place, tokens_keep, tokens_swap,
    )
    far_tokens = [swapped(block, top_mask) for block in send_tokens]
    (near,) = kernel_call(
        functools.partial(near_kernel, scale), "near", [f32(half_rows, width)], 12,
        place, near_tokens, cotangent, cotangent_swap,
    )
    projected, input_grad = kernel_call(
        project_kernel, "project", [f32(token_count, width)] * 2, 20, place, tokens, cotangent, weight,
        after=(near_tokens,),
    )
    weight_rows = lax.dynamic_slice_in_dim(weight, index * own, own, 0)
    near, projected, input_grad, weight_rows, far_mine, far_tokens[0] = lax.optimization_barrier(
        (near, projected, input_grad, weight_rows, far_mine, far_tokens[0])
    )
    far_main, far_rest = kernel_call(
        assemble_kernel, "assemble", [bf16(token_count, width)] * 2, 6, place, far_mine, swapped(far_mine, 1)
    )

    bits = list(range(levels - 2, 0, -1)) + [levels - 1]
    firsts = {}
    for message, far in zip(messages, far_tokens):
        for at, unit in enumerate(message):
            firsts[unit] = kernel_call(
                functools.partial(first_kernel, scale, bits[0], unit * unit_rows, at * unit_rows), "first",
                [f32(unit_rows // 2, width)] * 2, 8, place, near, far, far_main, far_rest,
            )
    state = [[firsts[unit] for unit in group] for group in groups]
    outs, after = {}, tuple(firsts[unit][0] for unit in range(units))
    order = [(k, level) for level in range(1, levels) for k in range(len(groups))]
    if len(groups) == 2 and levels == 5:
        order = ORDER
    arrived = [[swapped(send, 1 << bits[0]) for _, send in pairs] for pairs in state]
    after += tuple(block for blocks in arrived[1:] for block in blocks[:AHEAD])
    for k, level in order:
        count = len(groups[k])
        segment = unit_rows >> level
        operands = [place]
        for at, (keep, send) in enumerate(state[k]):
            operands += [keep, arrived[k][at] if level == 1 else swapped(send, 1 << bits[level - 1])]
        if level == levels - 1:
            outs[k] = kernel_call(
                functools.partial(last_kernel, streams[k]), "last", [f32(piece * count, width)] * 3, 4, *operands,
                weight_rows, first_moment, second_moment, after=after,
            )
            after = (outs[k][0],)
            continue
        made = kernel_call(
            functools.partial(middle_kernel, bits[level], segment), "middle",
            [f32(segment // 2 * count, width)] * 2, 8, *operands, after=after,
        )
        state[k] = [made]
        after = (made[0],)
    outs = [outs[k] for k in range(len(groups))]
    new_rows, new_first, new_second = zip(*outs)
    new_first = jnp.concatenate(new_first, axis=0)
    new_second = jnp.concatenate(new_second, axis=0)

    if devices > 64:
        mine = jnp.concatenate(new_rows, axis=0)
        new_weight = lax.all_gather(mine, "dp", axis=0, tiled=True)
        next_projected = jnp.dot(
            tokens, new_weight, precision=lax.Precision.HIGH, preferred_element_type=jnp.float32
        )
        return (projected, input_grad, new_weight, new_first, new_second, next_projected)

    order = list(range(levels - 2, 0, -1))
    load = dict.fromkeys(order, 0)
    blocks = []
    if JOIN:
        streams, sets = [sum(streams, [])], [list(new_rows)]
    else:
        sets = [[rows] for rows in new_rows]
    for at, rows in enumerate(sets):
        (both,) = kernel_call(
            pair_kernel, "pair", [f32(2 * sum(block.shape[0] for block in rows), width)], 4, place,
            *rows, *(swapped(block, top_mask) for block in rows),
        )
        if FRESH:
            load = dict.fromkeys(order, 0)
        found = relative_blocks(both, order, load, at >= DIRECT)
        for mid in range(middle):
            blocks += [found[mid << 1], swapped(found[mid << 1], 1)]
    new_weight, next_projected = kernel_call(
        functools.partial(finish_kernel, middle, own, streams), "finish",
        [f32(width, width), f32(token_count, width)], 28, place, tokens, *blocks,
    )
    return (projected, input_grad, new_weight, new_first, new_second, next_projected)


def solution(mesh):
    split, whole = P("dp", None), P()
    return jax.shard_map(
        on_device,
        mesh=mesh,
        in_specs=(split, split, whole, split, split),
        out_specs=(split, split, whole, split, split, split),
        check_vma=False,
    )
```

time: 142 us -> 137 us (0.965)
  waiting for transfers between devices: 42.3 us -> 72.5 us
  starting transfers between devices: 56.4 us -> 27.7 us
  Pallas kernels: 32.4 us -> 27.1 us
    ppermute x56 -> x33, waiting for transfers between devices: 42.3 us -> 72.5 us  [swapped(): lax.ppermute(block, 'dp', [(i, i ^ mask) for i in range(count) if owners...]
    ppermute x56 -> x33, starting transfers between devices: 56.4 us -> 27.7 us  [swapped(): lax.ppermute(block, 'dp', [(i, i ^ mask) for i in range(count) if owners...]
    pallas_call x27 -> x20, Pallas kernels: 32.4 us -> 27.1 us  [kernel_call(): pl.pallas_call(body, out_shape=tuple(outs), in_specs=[pl.BlockSpec(memory...]
    unnamed x28 -> x22, local copies, waits for them, and re-layouts: 7.85 us -> 7.22 us
  transfers between devices with their start and end apart: 56 -> 33, of which waited for: 20 -> 22; matrix products, arithmetic and copies ran while one was open for 1% -> 1% of each run, Pallas kernels for 20% -> 16%
where the time goes in v2:
time: 137 us
  waiting for transfers between devices  72.5 us (53%)
  starting transfers between devices  27.7 us (20%)
  Pallas kernels  27.1 us (20%)
  local copies, waits for them, and re-layouts  8.22 us (6%)
    ppermute x33, waiting for transfers between devices, swapped(): lax.ppermute(block, 'dp', [(i, i ^ mask) for i in range(count) if owners...  72.5 us
    ppermute x33, starting transfers between devices, swapped(): lax.ppermute(block, 'dp', [(i, i ^ mask) for i in range(count) if owners...  27.7 us
    pallas_call x20, Pallas kernels, kernel_call(): pl.pallas_call(body, out_shape=tuple(outs), in_specs=[pl.BlockSpec(memory...  27.1 us
    unnamed x22, local copies, waits for them, and re-layouts  7.22 us
  transfers between devices with their start and end apart: 33, of which 22 were waited for; matrix products, arithmetic and copies ran while one was open for 1% of the time, Pallas kernels for 16%

profile of v2, /device:TPU:0, one launch (start us, length us, event | category | flops | bytes accessed | tf_op | source)
XLA Modules:
  0.0 137.1 jit_solution(9661607270731170641)
XLA Ops:
  6.3 4.0 %collective-permute-start.2 = (f32[128,1024]{1,0:T(8,128)}, f32[128,1024]{1,0:T(8,128)}, u32[]{:S(2)}, u32[]{:S(2)}) collective-permute-start(f32[128,1024]{1,0:T(8,128)} %choose.1), channel_id=1, source_target_pairs={{0,16},{1,17},{2,18},{3,19},{4,20},{5,21},{6,22},{7,23},{8,24},{9,... | collective-permute-start | bytes 1572872 | tf_op jit(solution)/shard_map/ppermute | solution.py:57
  13.4 2.2 %copy-done.4 = f32[1024,1024]{1,0:T(8,128)S(1)} copy-done((f32[1024,1024]{1,0:T(8,128)S(1)}, f32[1024,1024]{1,0:T(8,128)}, u32[]{:S(2)}) %copy-start.4) | copy-done | bytes 4194328
  16.6 5.3 %project.1 = (f32[256,1024]{1,0:T(8,128)}, f32[256,1024]{1,0:T(8,128)}) custom-call(s32[9]{0:T(128)S(1)} %stack.43.refs_0_, f32[256,1024]{1,0:T(8,128)S(1)} %copy-done.3, f32[256,1024]{1,0:T(8,128)S(1)} %copy-done.1, f32[1024,1024]{1,0:T(8,128)S(1)} %copy-done.4, f32[512,256]{1,0:T(8,128)S(1)} %copy-done.6), custom_call_target="tpu_custom_call" | custom-call | flops 1 | bytes 1 | tf_op jit(solution)/shard_map/project/pallas_call | solution.py:33
  23.5 16.1 %collective-permute-done.3.refs_2_ = f32[128,256]{1,0:T(8,128)S(1)} collective-permute-done((f32[128,256]{1,0:T(8,128)S(1)}, f32[128,256]{1,0:T(8,128)S(1)}, u32[]{:S(2)}, u32[]{:S(2)}) %collective-permute-start.3) | collective-permute-done | bytes 131104 | tf_op jit(solution)/shard_map/ppermute | solution.py:57
  39.6 2.0 %collective-permute-done.4.refs_2_ = f32[128,1024]{1,0:T(8,128)S(1)} collective-permute-done((f32[128,1024]{1,0:T(8,128)}, f32[128,1024]{1,0:T(8,128)S(1)}, u32[]{:S(2)}, u32[]{:S(2)}) %collective-permute-start.4) | collective-permute-done | bytes 524320 | tf_op jit(solution)/shard_map/ppermute | solution.py:57
  44.2 2.1 %collective-permute-start.5 = (f32[64,1024]{1,0:T(8,128)S(1)}, f32[64,1024]{1,0:T(8,128)S(1)}, u32[]{:S(2)}, u32[]{:S(2)}) collective-permute-start(f32[64,1024]{1,0:T(8,128)S(1)} %get-tuple-element.63), channel_id=1, source_target_pairs={{0,8},{1,9},{2,10},{3,11},{4,12},{5,13},{6,14},{7,15},{8,0},{9,1},... | collective-permute-start | bytes 786440 | tf_op jit(solution)/shard_map/ppermute | solution.py:57
  46.4 14.1 %collective-permute-done.6.refs_2_ = f32[384,256]{1,0:T(8,128)S(1)} collective-permute-done((f32[384,256]{1,0:T(8,128)S(1)}, f32[384,256]{1,0:T(8,128)S(1)}, u32[]{:S(2)}, u32[]{:S(2)}) %collective-permute-start.6) | collective-permute-done | bytes 393248 | tf_op jit(solution)/shard_map/ppermute | solution.py:57
  63.2 2.1 %collective-permute-start.8 = (f32[64,1024]{1,0:T(8,128)S(1)}, f32[64,1024]{1,0:T(8,128)S(1)}, u32[]{:S(2)}, u32[]{:S(2)}) collective-permute-start(f32[64,1024]{1,0:T(8,128)S(1)} %get-tuple-element.69), channel_id=1, source_target_pairs={{0,8},{1,9},{2,10},{3,11},{4,12},{5,13},{6,14},{7,15},{8,0},{9,1},... | collective-permute-start | bytes 786440 | tf_op jit(solution)/shard_map/ppermute | solution.py:57
  66.7 4.3 %collective-permute-done.7.refs_4_ = f32[64,1024]{1,0:T(8,128)S(1)} collective-permute-done((f32[64,1024]{1,0:T(8,128)S(1)}, f32[64,1024]{1,0:T(8,128)S(1)}, u32[]{:S(2)}, u32[]{:S(2)}) %collective-permute-start.7) | collective-permute-done | bytes 262176 | tf_op jit(solution)/shard_map/ppermute | solution.py:57
  71.1 5.6 %collective-permute-done.8.refs_9_.refs_2_ = f32[64,1024]{1,0:T(8,128)S(1)} collective-permute-done((f32[64,1024]{1,0:T(8,128)S(1)}, f32[64,1024]{1,0:T(8,128)S(1)}, u32[]{:S(2)}, u32[]{:S(2)}) %collective-permute-start.8) | collective-permute-done | bytes 262176 | tf_op jit(solution)/shard_map/ppermute | solution.py:57
  77.5 1.6 %collective-permute-start.9 = (f32[64,1024]{1,0:T(8,128)S(1)}, f32[64,1024]{1,0:T(8,128)S(1)}, u32[]{:S(2)}, u32[]{:S(2)}) collective-permute-start(f32[64,1024]{1,0:T(8,128)S(1)} %get-tuple-element.71), channel_id=1, source_target_pairs={{0,4},{1,5},{2,6},{3,7},{4,0},{5,1},{6,2},{7,3},{8,12},{9,13},{10,... | collective-permute-start | bytes 786440 | tf_op jit(solution)/shard_map/ppermute | solution.py:57
  79.1 1.8 %collective-permute-done.10.refs_4_ = f32[64,1024]{1,0:T(8,128)S(1)} collective-permute-done((f32[64,1024]{1,0:T(8,128)S(1)}, f32[64,1024]{1,0:T(8,128)S(1)}, u32[]{:S(2)}, u32[]{:S(2)}) %collective-permute-start.10) | collective-permute-done | bytes 262176 | tf_op jit(solution)/shard_map/ppermute | solution.py:57
  81.7 1.6 %collective-permute-start.12 = (f32[64,1024]{1,0:T(8,128)S(1)}, f32[64,1024]{1,0:T(8,128)S(1)}, u32[]{:S(2)}, u32[]{:S(2)}) collective-permute-start(f32[64,1024]{1,0:T(8,128)S(1)} %get-tuple-element.76), channel_id=1, source_target_pairs={{0,4},{1,5},{2,6},{3,7},{4,0},{5,1},{6,2},{7,3},{8,12},{9,13},{10,... | collective-permute-start | bytes 786440 | tf_op jit(solution)/shard_map/ppermute | solution.py:57
  87.0 2.5 %collective-permute-done.12.refs_2_ = f32[64,1024]{1,0:T(8,128)S(1)} collective-permute-done((f32[64,1024]{1,0:T(8,128)S(1)}, f32[64,1024]{1,0:T(8,128)S(1)}, u32[]{:S(2)}, u32[]{:S(2)}) %collective-permute-start.12) | collective-permute-done | bytes 262176 | tf_op jit(solution)/shard_map/ppermute | solution.py:57
  92.9 2.3 %collective-permute-done.14.refs_2_ = f32[32,1024]{1,0:T(8,128)S(1)} collective-permute-done((f32[32,1024]{1,0:T(8,128)S(1)}, f32[32,1024]{1,0:T(8,128)S(1)}, u32[]{:S(2)}, u32[]{:S(2)}) %collective-permute-start.14) | collective-permute-done | bytes 131104 | tf_op jit(solution)/shard_map/ppermute | solution.py:57
  96.4 2.5 %collective-permute-done.13.refs_2_ = f32[16,1024]{1,0:T(8,128)S(1)} collective-permute-done((f32[16,1024]{1,0:T(8,128)S(1)}, f32[16,1024]{1,0:T(8,128)S(1)}, u32[]{:S(2)}, u32[]{:S(2)}) %collective-permute-start.13) | collective-permute-done | bytes 65568 | tf_op jit(solution)/shard_map/ppermute | solution.py:57
  99.6 1.7 %collective-permute-done.15.refs_2_ = f32[16,1024]{1,0:T(8,128)S(1)} collective-permute-done((f32[16,1024]{1,0:T(8,128)S(1)}, f32[16,1024]{1,0:T(8,128)S(1)}, u32[]{:S(2)}, u32[]{:S(2)}) %collective-permute-start.15) | collective-permute-done | bytes 65568 | tf_op jit(solution)/shard_map/ppermute | solution.py:57
  102.4 2.6 %collective-permute-start.16 = (f32[16,1024]{1,0:T(8,128)S(1)}, f32[16,1024]{1,0:T(8,128)S(1)}, u32[]{:S(2)}, u32[]{:S(2)}) collective-permute-start(f32[16,1024]{1,0:T(8,128)S(1)} %get-tuple-element.83.refs_6_.refs_1_), channel_id=1, source_target_pairs={{0,16},{1,17},{2,18},{3,19},{4,20},{5,21},{6,22},{7,23},{8,24},{9,... | collective-permute-start | bytes 196616 | tf_op jit(solution)/shard_map/ppermute | solution.py:57
  105.0 2.2 %collective-permute-done.17.refs_4_ = f32[16,1024]{1,0:T(8,128)S(1)} collective-permute-done((f32[16,1024]{1,0:T(8,128)S(1)}, f32[16,1024]{1,0:T(8,128)S(1)}, u32[]{:S(2)}, u32[]{:S(2)}) %collective-permute-start.17) | collective-permute-done | bytes 65568 | tf_op jit(solution)/shard_map/ppermute | solution.py:57
  108.5 3.8 %collective-permute-start.31 = (f32[64,1024]{1,0:T(8,128)S(1)}, f32[64,1024]{1,0:T(8,128)S(1)}, u32[]{:S(2)}, u32[]{:S(2)}) collective-permute-start(f32[64,1024]{1,0:T(8,128)S(1)} %pair.1.refs_2_), channel_id=1, source_target_pairs={{0,14},{1,15},{2,12},{3,13},{4,10},{5,11},{6,8},{7,9},{8,6},{9,7},... | collective-permute-start | bytes 786440 | tf_op jit(solution)/shard_map/ppermute | solution.py:57
  113.5 5.3 %collective-permute-done.31.refs_16_ = f32[64,1024]{1,0:T(8,128)S(1)} collective-permute-done((f32[64,1024]{1,0:T(8,128)S(1)}, f32[64,1024]{1,0:T(8,128)S(1)}, u32[]{:S(2)}, u32[]{:S(2)}) %collective-permute-start.31) | collective-permute-done | bytes 262176 | tf_op jit(solution)/shard_map/ppermute | solution.py:57
  123.6 3.9 %collective-permute-done.29.refs_14_ = f32[64,1024]{1,0:T(8,128)S(1)} collective-permute-done((f32[64,1024]{1,0:T(8,128)S(1)}, f32[64,1024]{1,0:T(8,128)S(1)}, u32[]{:S(2)}, u32[]{:S(2)}) %collective-permute-start.29) | collective-permute-done | bytes 262176 | tf_op jit(solution)/shard_map/ppermute | solution.py:57
  128.1 2.1 %collective-permute-done.23.refs_8_ = f32[64,1024]{1,0:T(8,128)S(1)} collective-permute-done((f32[64,1024]{1,0:T(8,128)S(1)}, f32[64,1024]{1,0:T(8,128)S(1)}, u32[]{:S(2)}, u32[]{:S(2)}) %collective-permute-start.23) | collective-permute-done | bytes 262176 | tf_op jit(solution)/shard_map/ppermute | solution.py:57
  132.6 4.5 %finish.1 = (f32[1024,1024]{1,0:T(8,128)}, f32[256,1024]{1,0:T(8,128)}) custom-call(s32[9]{0:T(128)S(1)} %stack.43.refs_0_, f32[256,1024]{1,0:T(8,128)S(1)} %copy-done.3, f32[64,1024]{1,0:T(8,128)S(1)} %pair.1.refs_2_, f32[64,1024]{1,0:T(8,128)S(1)} %collective-permute-done.18.refs_3_, f32[64,1024]{1,0:T(8,128)S(1)} %collective-permute-done.19.refs_4_, ...), custom_call_target="tpu_custom_call" | custom-call | flops 1 | bytes 1 | tf_op jit(solution)/shard_map/finish/pallas_call | solution.py:33
  (87 shorter events, 40.0 us)
Async XLA Ops:
  3.4 6.9 %collective-permute-start = (f32[512,256]{1,0:T(8,128)S(1)}, f32[512,256]{1,0:T(8,128)S(1)}, u32[]{:S(2)}, u32[]{:S(2)}) collective-permute-start(f32[512,256]{1,0:T(8,128)S(1)} %get-tuple-element.50), channel_id=1, source_target_pairs={{0,1},{1,0},{2,3},{3,2},{4,5},{5,4},{6,7},{7,6},{8,9},{9,8},{10,11... | collective-permute-start | bytes 1572872 | tf_op jit(solution)/shard_map/ppermute | solution.py:57
  6.3 33.2 %collective-permute-start.2 = (f32[128,1024]{1,0:T(8,128)}, f32[128,1024]{1,0:T(8,128)}, u32[]{:S(2)}, u32[]{:S(2)}) collective-permute-start(f32[128,1024]{1,0:T(8,128)} %choose.1), channel_id=1, source_target_pairs={{0,16},{1,17},{2,18},{3,19},{4,20},{5,21},{6,22},{7,23},{8,24},{9,... | collective-permute-start | bytes 1572872 | tf_op jit(solution)/shard_map/ppermute | solution.py:57
  12.4 27.1 %collective-permute-start.3 = (f32[128,256]{1,0:T(8,128)S(1)}, f32[128,256]{1,0:T(8,128)S(1)}, u32[]{:S(2)}, u32[]{:S(2)}) collective-permute-start(f32[128,256]{1,0:T(8,128)S(1)} %get-tuple-element.54), channel_id=1, source_target_pairs={{0,16},{1,17},{2,18},{3,19},{4,20},{5,21},{6,22},{7,23},{8,24},{9,... | collective-permute-start | bytes 393224 | tf_op jit(solution)/shard_map/ppermute | solution.py:57
  39.5 20.9 %collective-permute-start.6 = (f32[384,256]{1,0:T(8,128)S(1)}, f32[384,256]{1,0:T(8,128)S(1)}, u32[]{:S(2)}, u32[]{:S(2)}) collective-permute-start(f32[384,256]{1,0:T(8,128)S(1)} %copy-done.10), channel_id=1, source_target_pairs={{0,16},{1,17},{2,18},{3,19},{4,20},{5,21},{6,22},{7,23},{8,24},{9,... | collective-permute-start | bytes 1179656 | tf_op jit(solution)/shard_map/ppermute | solution.py:57
  44.2 22.5 %collective-permute-start.5 = (f32[64,1024]{1,0:T(8,128)S(1)}, f32[64,1024]{1,0:T(8,128)S(1)}, u32[]{:S(2)}, u32[]{:S(2)}) collective-permute-start(f32[64,1024]{1,0:T(8,128)S(1)} %get-tuple-element.63), channel_id=1, source_target_pairs={{0,8},{1,9},{2,10},{3,11},{4,12},{5,13},{6,14},{7,15},{8,0},{9,1},... | collective-permute-start | bytes 786440 | tf_op jit(solution)/shard_map/ppermute | solution.py:57
  61.8 9.3 %collective-permute-start.7 = (f32[64,1024]{1,0:T(8,128)S(1)}, f32[64,1024]{1,0:T(8,128)S(1)}, u32[]{:S(2)}, u32[]{:S(2)}) collective-permute-start(f32[64,1024]{1,0:T(8,128)S(1)} %get-tuple-element.66), channel_id=1, source_target_pairs={{0,8},{1,9},{2,10},{3,11},{4,12},{5,13},{6,14},{7,15},{8,0},{9,1},... | collective-permute-start | bytes 786440 | tf_op jit(solution)/shard_map/ppermute | solution.py:57
  63.2 13.5 %collective-permute-start.8 = (f32[64,1024]{1,0:T(8,128)S(1)}, f32[64,1024]{1,0:T(8,128)S(1)}, u32[]{:S(2)}, u32[]{:S(2)}) collective-permute-start(f32[64,1024]{1,0:T(8,128)S(1)} %get-tuple-element.69), channel_id=1, source_target_pairs={{0,8},{1,9},{2,10},{3,11},{4,12},{5,13},{6,14},{7,15},{8,0},{9,1},... | collective-permute-start | bytes 786440 | tf_op jit(solution)/shard_map/ppermute | solution.py:57
  66.6 14.3 %collective-permute-start.10 = (f32[64,1024]{1,0:T(8,128)S(1)}, f32[64,1024]{1,0:T(8,128)S(1)}, u32[]{:S(2)}, u32[]{:S(2)}) collective-permute-start(f32[64,1024]{1,0:T(8,128)S(1)} %get-tuple-element.72), channel_id=1, source_target_pairs={{0,8},{1,9},{2,10},{3,11},{4,12},{5,13},{6,14},{7,15},{8,0},{9,1},... | collective-permute-start | bytes 786440 | tf_op jit(solution)/shard_map/ppermute | solution.py:57
  77.5 7.3 %collective-permute-start.9 = (f32[64,1024]{1,0:T(8,128)S(1)}, f32[64,1024]{1,0:T(8,128)S(1)}, u32[]{:S(2)}, u32[]{:S(2)}) collective-permute-start(f32[64,1024]{1,0:T(8,128)S(1)} %get-tuple-element.71), channel_id=1, source_target_pairs={{0,4},{1,5},{2,6},{3,7},{4,0},{5,1},{6,2},{7,3},{8,12},{9,13},{10,... | collective-permute-start | bytes 786440 | tf_op jit(solution)/shard_map/ppermute | solution.py:57
  81.7 7.9 %collective-permute-start.12 = (f32[64,1024]{1,0:T(8,128)S(1)}, f32[64,1024]{1,0:T(8,128)S(1)}, u32[]{:S(2)}, u32[]{:S(2)}) collective-permute-start(f32[64,1024]{1,0:T(8,128)S(1)} %get-tuple-element.76), channel_id=1, source_target_pairs={{0,4},{1,5},{2,6},{3,7},{4,0},{5,1},{6,2},{7,3},{8,12},{9,13},{10,... | collective-permute-start | bytes 786440 | tf_op jit(solution)/shard_map/ppermute | solution.py:57
  85.5 6.4 %collective-permute-start.11 = (f32[32,1024]{1,0:T(8,128)S(1)}, f32[32,1024]{1,0:T(8,128)S(1)}, u32[]{:S(2)}, u32[]{:S(2)}) collective-permute-start(f32[32,1024]{1,0:T(8,128)S(1)} %get-tuple-element.75), channel_id=1, source_target_pairs={{0,2},{1,3},{2,0},{3,1},{4,6},{5,7},{6,4},{7,5},{8,10},{9,11},{10,... | collective-permute-start | bytes 393224 | tf_op jit(solution)/shard_map/ppermute | solution.py:57
  92.5 6.4 %collective-permute-start.13 = (f32[16,1024]{1,0:T(8,128)S(1)}, f32[16,1024]{1,0:T(8,128)S(1)}, u32[]{:S(2)}, u32[]{:S(2)}) collective-permute-start(f32[16,1024]{1,0:T(8,128)S(1)} %get-tuple-element.79), channel_id=1, source_target_pairs={{0,16},{1,17},{2,18},{3,19},{4,20},{5,21},{6,22},{7,23},{8,24},{9,... | collective-permute-start | bytes 196616 | tf_op jit(solution)/shard_map/ppermute | solution.py:57
  95.9 5.3 %collective-permute-start.15 = (f32[16,1024]{1,0:T(8,128)S(1)}, f32[16,1024]{1,0:T(8,128)S(1)}, u32[]{:S(2)}, u32[]{:S(2)}) collective-permute-start(f32[16,1024]{1,0:T(8,128)S(1)} %get-tuple-element.84), channel_id=1, source_target_pairs={{0,16},{1,17},{2,18},{3,19},{4,20},{5,21},{6,22},{7,23},{8,24},{9,... | collective-permute-start | bytes 196616 | tf_op jit(solution)/shard_map/ppermute | solution.py:57
  102.4 5.5 %collective-permute-start.16 = (f32[16,1024]{1,0:T(8,128)S(1)}, f32[16,1024]{1,0:T(8,128)S(1)}, u32[]{:S(2)}, u32[]{:S(2)}) collective-permute-start(f32[16,1024]{1,0:T(8,128)S(1)} %get-tuple-element.83.refs_6_.refs_1_), channel_id=1, source_target_pairs={{0,16},{1,17},{2,18},{3,19},{4,20},{5,21},{6,22},{7,23},{8,24},{9,... | collective-permute-start | bytes 196616 | tf_op jit(solution)/shard_map/ppermute | solution.py:57
  108.5 10.3 %collective-permute-start.31 = (f32[64,1024]{1,0:T(8,128)S(1)}, f32[64,1024]{1,0:T(8,128)S(1)}, u32[]{:S(2)}, u32[]{:S(2)}) collective-permute-start(f32[64,1024]{1,0:T(8,128)S(1)} %pair.1.refs_2_), channel_id=1, source_target_pairs={{0,14},{1,15},{2,12},{3,13},{4,10},{5,11},{6,8},{7,9},{8,6},{9,7},... | collective-permute-start | bytes 786440 | tf_op jit(solution)/shard_map/ppermute | solution.py:57
  112.3 7.9 %collective-permute-start.25 = (f32[64,1024]{1,0:T(8,128)S(1)}, f32[64,1024]{1,0:T(8,128)S(1)}, u32[]{:S(2)}, u32[]{:S(2)}) collective-permute-start(f32[64,1024]{1,0:T(8,128)S(1)} %pair.1.refs_2_), channel_id=1, source_target_pairs={{0,8},{1,9},{2,10},{3,11},{4,12},{5,13},{6,14},{7,15},{8,0},{9,1},... | collective-permute-start | bytes 786440 | tf_op jit(solution)/shard_map/ppermute | solution.py:57
  112.5 9.0 %collective-permute-start.21 = (f32[64,1024]{1,0:T(8,128)S(1)}, f32[64,1024]{1,0:T(8,128)S(1)}, u32[]{:S(2)}, u32[]{:S(2)}) collective-permute-start(f32[64,1024]{1,0:T(8,128)S(1)} %pair.1.refs_2_), channel_id=1, source_target_pairs={{0,4},{1,5},{2,6},{3,7},{4,0},{5,1},{6,2},{7,3},{8,12},{9,13},{10,... | collective-permute-start | bytes 786440 | tf_op jit(solution)/shard_map/ppermute | solution.py:57
  113.0 8.6 %collective-permute-start.19 = (f32[64,1024]{1,0:T(8,128)S(1)}, f32[64,1024]{1,0:T(8,128)S(1)}, u32[]{:S(2)}, u32[]{:S(2)}) collective-permute-start(f32[64,1024]{1,0:T(8,128)S(1)} %pair.1.refs_2_), channel_id=1, source_target_pairs={{0,2},{1,3},{2,0},{3,1},{4,6},{5,7},{6,4},{7,5},{8,10},{9,11},{10,... | collective-permute-start | bytes 786440 | tf_op jit(solution)/shard_map/ppermute | solution.py:57
  113.5 9.2 %collective-permute-start.18 = (f32[64,1024]{1,0:T(8,128)S(1)}, f32[64,1024]{1,0:T(8,128)S(1)}, u32[]{:S(2)}, u32[]{:S(2)}) collective-permute-start(f32[64,1024]{1,0:T(8,128)S(1)} %pair.1.refs_2_), channel_id=1, source_target_pairs={{0,1},{1,0},{2,3},{3,2},{4,5},{5,4},{6,7},{7,6},{8,9},{9,8},{10,11... | collective-permute-start | bytes 786440 | tf_op jit(solution)/shard_map/ppermute | solution.py:57
  120.1 7.4 %collective-permute-start.29 = (f32[64,1024]{1,0:T(8,128)S(1)}, f32[64,1024]{1,0:T(8,128)S(1)}, u32[]{:S(2)}, u32[]{:S(2)}) collective-permute-start(f32[64,1024]{1,0:T(8,128)S(1)} %collective-permute-done.25.refs_10_), channel_id=1, source_target_pairs={{0,4},{1,5},{2,6},{3,7},{4,0},{5,1},{6,2},{7,3},{8,12},{9,13},{10,... | collective-permute-start | bytes 786440 | tf_op jit(solution)/shard_map/ppermute | solution.py:57
  121.5 6.1 %collective-permute-start.26 = (f32[64,1024]{1,0:T(8,128)S(1)}, f32[64,1024]{1,0:T(8,128)S(1)}, u32[]{:S(2)}, u32[]{:S(2)}) collective-permute-start(f32[64,1024]{1,0:T(8,128)S(1)} %collective-permute-done.25.refs_10_), channel_id=1, source_target_pairs={{0,1},{1,0},{2,3},{3,2},{4,5},{5,4},{6,7},{7,6},{8,9},{9,8},{10,11... | collective-permute-start | bytes 786440 | tf_op jit(solution)/shard_map/ppermute | solution.py:57
  121.6 8.6 %collective-permute-start.23 = (f32[64,1024]{1,0:T(8,128)S(1)}, f32[64,1024]{1,0:T(8,128)S(1)}, u32[]{:S(2)}, u32[]{:S(2)}) collective-permute-start(f32[64,1024]{1,0:T(8,128)S(1)} %collective-permute-done.21.refs_6_), channel_id=1, source_target_pairs={{0,2},{1,3},{2,0},{3,1},{4,6},{5,7},{6,4},{7,5},{8,10},{9,11},{10,... | collective-permute-start | bytes 786440 | tf_op jit(solution)/shard_map/ppermute | solution.py:57
  122.7 8.4 %collective-permute-start.27 = (f32[64,1024]{1,0:T(8,128)S(1)}, f32[64,1024]{1,0:T(8,128)S(1)}, u32[]{:S(2)}, u32[]{:S(2)}) collective-permute-start(f32[64,1024]{1,0:T(8,128)S(1)} %collective-permute-done.19.refs_4_), channel_id=1, source_target_pairs={{0,8},{1,9},{2,10},{3,11},{4,12},{5,13},{6,14},{7,15},{8,0},{9,1},... | collective-permute-start | bytes 786440 | tf_op jit(solution)/shard_map/ppermute | solution.py:57
  123.6 8.2 %collective-permute-start.22 = (f32[64,1024]{1,0:T(8,128)S(1)}, f32[64,1024]{1,0:T(8,128)S(1)}, u32[]{:S(2)}, u32[]{:S(2)}) collective-permute-start(f32[64,1024]{1,0:T(8,128)S(1)} %collective-permute-done.21.refs_6_), channel_id=1, source_target_pairs={{0,1},{1,0},{2,3},{3,2},{4,5},{5,4},{6,7},{7,6},{8,9},{9,8},{10,11... | collective-permute-start | bytes 786440 | tf_op jit(solution)/shard_map/ppermute | solution.py:57
  (20 other events, 154.6 us)
